TPU v7x, 256 devices: a whole 4x4x8 slice. The times are simulated.
256 devices in a mesh: dap: 64 (over x, z, core), blk: 4 (over y).
Axes of the slice: x: 4, y: 4, z: 8, core: 2. Of those that a mesh axis runs over, the one named last changes fastest.
Arguments:
- coevolution_profile_tensor: bfloat16 [512, 512, 256], P('blk', 'dap'), may hold values from -60 to 60
- residue_couple_embedding: bfloat16 [512, 512, 128], P('dap'), may hold values from -0.47851562 to 0.47851562
- leftward_aggregate_vector: bfloat16 [256, 32], replicated, may hold values from -0.375 to 0.375
- starboard_pooled_factor: bfloat16 [256, 32], replicated, may hold values from -0.375 to 0.375
- average_final_matrix: bfloat16 [1024, 128], replicated, may hold values from -0.1875 to 0.1875
- first_edge_sigmoid: bfloat16 [128, 128], replicated, may hold values from -0.5 to 0.5
- first_edge_matrix: bfloat16 [128, 128], replicated, may hold values from -0.5 to 0.5
- second_edge_sigmoid: bfloat16 [128, 128], replicated, may hold values from -0.5 to 0.5
- latter_pairing_grid: bfloat16 [128, 128], replicated, may hold values from -0.5 to 0.5
- edge_final_sigmoid: bfloat16 [128, 128], replicated, may hold values from -0.5 to 0.5
- edge_final_matrix: bfloat16 [128, 128], replicated, may hold values from -0.5 to 0.5
Outputs:
- pair_out: bfloat16 [512, 512, 128], P('dap', 'blk')
All inputs are finite; a program needn't handle non-finite values.
Results may differ from a plain program's by a relative error of at most 0.03.
Values may be sent and summed in bfloat16 or wider, within the bound.
A program may use at most 128 MiB of HBM per device.

v0:
```python
import jax
import jax.numpy as jnp
from jax import lax
from jax.sharding import PartitionSpec as P


def zscore_channelwise(values, axis):
    mean = jnp.mean(values, axis=axis, keepdims=True)
    centered = values - mean
    var = jnp.mean(centered * centered, axis=axis, keepdims=True)
    return centered * lax.rsqrt(var + 1e-05)


def gated_last(values, gate_weight, proj_weight):
    gate_part = jnp.einsum("ikd,dc->ikc", values, gate_weight, preferred_element_type=jnp.float32)
    proj_part = jnp.einsum("ikd,dc->ikc", values, proj_weight, preferred_element_type=jnp.float32)
    return (jax.nn.sigmoid(gate_part) * proj_part).astype(jnp.bfloat16)


def shards(
    coevolution_profile_tensor,
    residue_couple_embedding,
    leftward_aggregate_vector,
    starboard_pooled_factor,
    average_final_matrix,
    first_edge_sigmoid,
    first_edge_matrix,
    second_edge_sigmoid,
    latter_pairing_grid,
    edge_final_sigmoid,
    edge_final_matrix,
):
    evoformer_units = lax.axis_size("blk")
    column = lax.axis_index("blk")
    length = residue_couple_embedding.shape[1]
    width = length // evoformer_units
    related_chain_tally = coevolution_profile_tensor.shape[0] * evoformer_units
    weighted_covariation_array = zscore_channelwise(
        coevolution_profile_tensor.astype(jnp.float32), 2
    ).astype(jnp.bfloat16)
    port_operand = jnp.einsum(
        "icr,rx->cix",
        weighted_covariation_array,
        leftward_aggregate_vector,
        preferred_element_type=jnp.float32,
    ).astype(jnp.bfloat16)
    rightward_multiplicand = jnp.einsum(
        "hgq,qa->hag",
        weighted_covariation_array,
        starboard_pooled_factor,
        preferred_element_type=jnp.float32,
    ).astype(jnp.bfloat16)
    outer_weight = average_final_matrix.astype(jnp.float32)
    piece = lax.all_gather(rightward_multiplicand, "dap", axis=2, tiled=True)

    def one_row(left_row):
        product = jnp.einsum("sc,ser->rce", left_row, piece, preferred_element_type=jnp.float32)
        flat = product.reshape(product.shape[0], product.shape[1] * product.shape[2])
        return jnp.dot(
            flat, outer_weight, precision=lax.Precision.HIGHEST, preferred_element_type=jnp.float32
        )

    incomplete_accumuland = lax.map(one_row, port_operand)
    offset = column * width
    summed = lax.psum(incomplete_accumuland.astype(jnp.bfloat16), "blk").astype(jnp.float32)
    updated = (residue_couple_embedding.astype(jnp.float32) + summed / related_chain_tally).astype(
        jnp.bfloat16
    )
    own_updated = lax.dynamic_slice_in_dim(updated, offset, width, 1)
    own_norm = zscore_channelwise(own_updated.astype(jnp.float32), 2).astype(jnp.bfloat16)
    lhs = gated_last(own_norm, first_edge_sigmoid, first_edge_matrix)
    rhs = gated_last(own_norm, second_edge_sigmoid, latter_pairing_grid)
    partial_mixed = jnp.einsum(
        "ikc,jkc->icj",
        lhs,
        lax.all_gather(rhs, "dap", axis=0, tiled=True),
        preferred_element_type=jnp.float32,
    )
    mixed = lax.psum_scatter(
        partial_mixed.astype(jnp.bfloat16), "blk", scatter_dimension=2, tiled=True
    ).astype(jnp.float32)
    mixed_norm = zscore_channelwise(mixed, 1).astype(jnp.bfloat16)
    projected = jnp.einsum(
        "icj,cd->ijd", mixed_norm, edge_final_matrix, preferred_element_type=jnp.float32
    )
    gate = jax.nn.sigmoid(
        jnp.einsum("ijd,de->ije", own_norm, edge_final_sigmoid, preferred_element_type=jnp.float32)
    )
    return (own_updated.astype(jnp.float32) + gate * projected).astype(jnp.bfloat16)


def solution(mesh):
    placed = (
        P("blk", "dap", None),
        P("dap", None, None),
        P(),
        P(),
        P(),
        P(),
        P(),
        P(),
        P(),
        P(),
        P(),
    )
    return jax.shard_map(
        shards, mesh=mesh, in_specs=placed, out_specs=P("dap", "blk", None), check_vma=False
    )
```

profile of v0, /device:TPU:1, one launch (start us, length us, event | category | flops | bytes accessed | tf_op | source)
XLA Modules:
  0.0 439.3 jit_solution(13083277325017985919)
XLA Ops:
  6.5 1.3 convert_reduce_fusion
  7.9 1.4 fusion.22
  9.3 1.5 fusion.21
  10.8 0.8 copy.26
  11.7 1.5 fusion.20
  13.4 81.6 %all-gather.3.cloned.1.call-done = bf16[128,32,512]{0,1,2:T(8,128)(2,1)} async-done(((bf16[128,32,8]{0,1,2:T(8,128)(2,1)}), bf16[128,32,512]{0,1,2:T(8,128)(2,1)}) %all-gather.3.cloned.1.call-update) | async-done | bytes 4194320 | tf_op jit(solution)/shard_map/all_gather | solution.py:54
  95.0 7.6 %copy.28 = bf16[128,32,512]{2,0,1:T(8,128)(2,1)} copy(bf16[128,32,512]{0,1,2:T(8,128)(2,1)} %all-gather.3.cloned.1.call-done) | data formatting | bytes 8388608 | tf_op jit(solution)/shard_map/while | solution.py:63
  102.5 65.8 %while.10 = (s32[]{:T(128)}, bf16[8,512,128]{2,1,0:T(8,128)(2,1)}, bf16[8,128,32]{1,2,0:T(8,128)(2,1)S(1)}, bf16[128,32,512]{2,0,1:T(8,128)(2,1)}, f32[1024,128]{1,0:T(8,128)S(1)}, /*index=5*/s32[]{:T(128)}) while((s32[]{:T(128)}, bf16[8,512,128]{2,1,0:T(8,128)(2,1)}, bf16[8,128,32]{1,2,0:T(8,128)(2,1)S(1)}, bf16[128,32,512]{2,0,1:T(8,128)(2,1)}, ...), condition=%wide.region_3.4_spmd, body=%wide.region_2.3_spmd.sunk | while | flops 939524096 | bytes 13377621 | solution.py:63
  102.5 2.9 convolution_bitcast_fusion.3
  105.4 1.2 copy.37
  106.6 4.1 fusion.62
  110.8 2.9 convolution_bitcast_fusion.3
  113.6 1.2 copy.37
  114.9 4.1 fusion.62
  119.0 2.9 convolution_bitcast_fusion.3
  121.9 1.2 copy.37
  123.1 4.1 fusion.62
  127.2 2.9 convolution_bitcast_fusion.3
  130.1 1.2 copy.37
  131.3 4.1 fusion.62
  135.4 2.9 convolution_bitcast_fusion.3
  138.3 1.2 copy.37
  139.5 4.1 fusion.62
  143.7 2.9 convolution_bitcast_fusion.3
  146.6 1.2 copy.37
  147.8 4.1 fusion.62
  151.9 2.9 convolution_bitcast_fusion.3
  154.8 1.2 copy.37
  156.0 4.1 fusion.62
  160.2 2.9 convolution_bitcast_fusion.3
  163.0 1.2 copy.37
  164.2 4.1 fusion.62
  168.5 46.5 %all-reduce.2.cloned.1.call-done = bf16[8,512,128]{2,1,0:T(8,128)(2,1)} async-done(((bf16[8,512,128]{2,1,0:T(8,128)(2,1)}), bf16[8,512,128]{2,1,0:T(8,128)(2,1)}) %all-reduce.2.cloned.1.call-update) | async-done | bytes 1048592 | tf_op jit(solution)/shard_map/psum | solution.py:65
  215.0 1.2 convert_reduce_fusion.1
  216.6 0.7 fusion.12
  217.4 1.2 fusion.18
  218.8 0.7 fusion.9
  219.6 0.5 fusion.19
  220.2 100.9 %all-gather.5.cloned.1.call-done = bf16[512,128,128]{2,1,0:T(8,128)(2,1)} async-done(((bf16[8,128,128]{2,1,0:T(8,128)(2,1)}), bf16[512,128,128]{2,1,0:T(8,128)(2,1)}) %all-gather.5.cloned.1.call-update) | async-done | bytes 16777232 | tf_op jit(solution)/shard_map/all_gather | solution.py:76
  321.1 21.5 %copy.29 = bf16[512,128,128]{1,0,2:T(8,128)(2,1)} copy(bf16[512,128,128]{2,1,0:T(8,128)(2,1)} %all-gather.5.cloned.1.call-done) | data formatting | bytes 33554432 | tf_op jit(solution)/shard_map/all_gather | solution.py:76
  342.6 8.0 %fusion.4 = bf16[8,128,512]{2,0,1:T(8,128)(2,1)S(1)} fusion(bf16[512,128,128]{1,0,2:T(8,128)(2,1)} %copy.29, bf16[8,128,128]{1,0,2:T(8,128)(2,1)S(1)} %copy.30), kind=kOutput, calls=%fused_computation.7 | convolution fusion | flops 134742016 | bytes 18087936 | tf_op jit(solution)/shard_map/ikc,jkc->icj/dot_general | solution.py:73
  350.6 22.5 %copy.32 = bf16[8,128,512]{0,1,2:T(8,128)(2,1)} copy(bf16[8,128,512]{2,0,1:T(8,128)(2,1)S(1)} %fusion.4) | data formatting | bytes 2097152
  373.1 25.2 %reshape.48 = bf16[512,1024]{1,0:T(8,128)(2,1)} reshape(bf16[512,128,8]{2,1,0:T(8,128)(2,1)} %bitcast.64) | data formatting | bytes 2097152
  398.3 0.7 fusion.15
  399.0 20.0 %reduce-scatter.4.cloned.1.call-done = bf16[128,1024]{1,0:T(8,128)(2,1)} async-done(((bf16[512,1024]{1,0:T(8,128)(2,1)}), bf16[128,1024]{1,0:T(8,128)(2,1)}) %reduce-scatter.4.cloned.1.call-update) | async-done | bytes 262160
  419.1 6.8 %reshape.49 = bf16[128,128,8]{2,1,0:T(8,128)(2,1)} reshape(bf16[128,1024]{1,0:T(8,128)(2,1)} %reduce-scatter.4.cloned.1.call-done) | data formatting | bytes 524288
  425.9 5.4 %copy.33 = bf16[8,128,128]{2,0,1:T(8,128)(2,1)S(1)} copy(bf16[8,128,128]{0,1,2:T(8,128)(2,1)} %bitcast.65) | data formatting | bytes 524288
  431.8 1.0 fusion.17
  (38 shorter events, 1.6 us)
Async XLA Ops:
  6.5 210.1 %copy-start = (bf16[128,128]{1,0:T(8,128)(2,1)S(1)}, bf16[128,128]{1,0:T(8,128)(2,1)}, u32[]{:S(2)}) copy-start(bf16[128,128]{1,0:T(8,128)(2,1)} %param.20) | copy-start | bytes 98308
  6.5 6.8 %copy-start.2 = (bf16[1024,128]{1,0:T(8,128)(2,1)S(1)}, bf16[1024,128]{1,0:T(8,128)(2,1)}, u32[]{:S(2)}) copy-start(bf16[1024,128]{1,0:T(8,128)(2,1)} %param.17) | copy-start | bytes 786436
  6.5 88.4 %all-gather.3.cloned.1.call-start = ((), (), s32[]{:S(2)}) async-start(), calls=%async_computation.1 | async-start | bytes 4259840 | tf_op jit(solution)/shard_map/all_gather | solution.py:54
  11.6 203.4 %all-reduce.2.cloned.1.call-start = ((), (), s32[]{:S(2)}) async-start(), calls=%async_computation.2 | async-start | bytes 2097152 | tf_op jit(solution)/shard_map/psum | solution.py:65
  168.4 49.0 %copy-start.3 = (bf16[128,128]{1,0:T(8,128)(2,1)S(1)}, bf16[128,128]{1,0:T(8,128)(2,1)}, u32[]{:S(2)}) copy-start(bf16[128,128]{1,0:T(8,128)(2,1)} %param.21) | copy-start | bytes 98308
  168.4 50.4 %copy-start.6 = (bf16[128,128]{1,0:T(8,128)(2,1)S(1)}, bf16[128,128]{1,0:T(8,128)(2,1)}, u32[]{:S(2)}) copy-start(bf16[128,128]{1,0:T(8,128)(2,1)} %param.18) | copy-start | bytes 98308
  168.4 51.2 %copy-start.4 = (bf16[128,128]{1,0:T(8,128)(2,1)S(1)}, bf16[128,128]{1,0:T(8,128)(2,1)}, u32[]{:S(2)}) copy-start(bf16[128,128]{1,0:T(8,128)(2,1)} %param.19) | copy-start | bytes 98308
  168.4 152.7 %all-gather.5.cloned.1.call-start = ((), (), s32[]{:S(2)}) async-start(), calls=%async_computation.3 | async-start | bytes 17039360 | tf_op jit(solution)/shard_map/all_gather | solution.py:76
  218.6 200.5 %reduce-scatter.4.cloned.1.call-start = ((), (), s32[]{:S(2)}) async-start(), calls=%async_computation.4 | async-start | bytes 1310720
  373.1 25.2 %copy-start.7 = (bf16[128,128]{1,0:T(8,128)(2,1)S(1)}, bf16[128,128]{1,0:T(8,128)(2,1)}, u32[]{:S(2)}) copy-start(bf16[128,128]{1,0:T(8,128)(2,1)} %param.22) | copy-start | bytes 98308
  399.0 32.7 %copy-start.5 = (bf16[128,128]{1,0:T(8,128)(2,1)S(1)}, bf16[128,128]{1,0:T(8,128)(2,1)}, u32[]{:S(2)}) copy-start(bf16[128,128]{1,0:T(8,128)(2,1)} %param.23) | copy-start | bytes 98308
  419.1 13.7 %copy-start.1 = (bf16[128,128]{1,0:T(8,128)(2,1)S(1)}, bf16[128,128]{1,0:T(8,128)(2,1)}, u32[]{:S(2)}) copy-start(bf16[128,128]{1,0:T(8,128)(2,1)} %param.20) | copy-start | bytes 98308
Sparse Core Ops, SparseCore 0:
  11.8 83.1 all-gather.2
  168.5 46.3 all-reduce.1
  218.7 102.3 all-gather.4
  398.4 20.6 reduce-scatter.3
where the time goes:
time: 442 us; the launch traced here: 439 us
  waiting for transfers between devices  249 us (56%)
  local copies, waits for them, and re-layouts  100 us (23%)
  matrix products  71.8 us (16%)
  between operations  13.3 us (3%)
  other arithmetic  4.75 us (1%)
    all_gather x1, waiting for transfers between devices, shards(): lax.all_gather(rhs, 'dap', axis=0, tiled=True)  101 us
    all_gather x1, waiting for transfers between devices, shards(): piece = lax.all_gather(rightward_multiplicand, 'dap', axis=2, tiled=True)  81.6 us
    unnamed x20, local copies, waits for them, and re-layouts  60 us
    psum x1, waiting for transfers between devices, shards(): lax.psum(incomplete_accumuland.astype(jnp.bfloat16), 'blk')  46.5 us
    dot_general x8, matrix products, one_row(): jnp.dot(flat, outer_weight, precision=lax.Precision.HIGHEST, preferred_el...  33.1 us
    dot_general x8, matrix products, one_row(): jnp.einsum('sc,ser->rce', left_row, piece, preferred_element_type=jnp.flo...  22.9 us
    all_gather x1, local copies, waits for them, and re-layouts, shards(): lax.all_gather(rhs, 'dap', axis=0, tiled=True)  21.5 us
    unnamed x5, waiting for transfers between devices  20.1 us
  transfers between devices with their start and end apart: 4, of which 4 were waited for; matrix products, arithmetic and copies ran while one was open for 1% of the time, Pallas kernels for 0%

commit v1 on v0

v1 whole, which is shorter than its diff:
```python
import functools

import jax
import jax.numpy as jnp
from jax import lax
from jax.experimental import pallas as pl
from jax.experimental.pallas import tpu as pltpu
from jax.sharding import PartitionSpec as P

NZ = 8
NC = 2
ROWS = 8
EPS = 1e-5
MESH = pl.DeviceIdType.MESH
F32 = jnp.float32
BF16 = jnp.bfloat16


def nt(a, b):
    return lax.dot_general(a, b, (((1,), (1,)), ((), ())), preferred_element_type=F32)


def zscore(v, axis):
    centered = v - jnp.mean(v, axis=axis, keepdims=True)
    var = jnp.mean(centered * centered, axis=axis, keepdims=True)
    return centered * lax.rsqrt(var + EPS)


def device(x, y, z, c):
    return (x * NZ + z) * NC + c, y


def kernel(
    nx, ny, seqs,
    msa_ref, pair_ref, wl_ref, wr_ref, wo_ref, ag_ref, ap_ref, bg_ref, bp_ref, fg_ref, fp_ref,
    out_ref,
    xf, lscr, lsend, lbuf, rsend, rbuf, abuf, bd, tsend, tbuf, vbuf, pairv, upd, pn, wt4,
    lrscr, lrsend, lrbuf, lrsib, msend, mbuf, nscr, gates,
    pair_sem, lsem, rsem, csem, tsend_sem, trecv_sem, asem, ssem, msem,
):
    d = lax.axis_index("dap")
    y = lax.axis_index("blk")
    x, z, c = d // (NZ * NC), (d // NC) % NZ, d % NC
    sd = msa_ref.shape[0] // ROWS
    ch = wl_ref.shape[1]
    cz = wo_ref.shape[1]
    jr = ROWS // ny
    slab = 4
    njo = NZ * jr // slab
    width = NZ * NC * ROWS
    nxz = nx * NZ
    peers = nx * ny * NZ
    sibling = device(x, y, z, 1 - c)

    def peer(k):
        r = lax.rem(k, ny * NZ)
        x2 = lax.rem(x + lax.div(k, ny * NZ), nx)
        z2 = lax.rem(z + lax.div(r, ny), NZ)
        y2 = lax.rem(y + lax.rem(r, ny), ny)
        return x2, y2, z2

    def greet(k, carry):
        x2, y2, z2 = peer(k)
        pl.semaphore_signal(barrier, inc=1, device_id=device(x2, y2, z2, c), device_id_type=MESH)
        return carry

    barrier = pltpu.get_barrier_semaphore()
    pl.semaphore_signal(barrier, inc=1, device_id=sibling, device_id_type=MESH)
    lax.fori_loop(1, peers, greet, 0)

    pair_copy = pltpu.make_async_copy(
        pair_ref.at[:, pl.ds(pl.multiple_of(y * width, width), width), :], pairv, pair_sem
    )
    pair_copy.start()

    lanes = xf.shape[1]
    blocks = msa_ref.shape[1] // lanes
    for h in range(blocks):
        xf[h * sd * ROWS : (h + 1) * sd * ROWS] = msa_ref[:, h * lanes : (h + 1) * lanes].astype(F32)
    wlr = jnp.concatenate([wl_ref[...].astype(F32).T, wr_ref[...].astype(F32).T], axis=0).astype(BF16)
    for i in range(ROWS):
        v = jnp.concatenate(
            [xf[pl.ds(h * sd * ROWS + i, sd, stride=ROWS), :] for h in range(blocks)], axis=1
        )
        v = zscore(v, 1).astype(BF16)
        proj = nt(wlr, v)
        lscr[pl.ds(i, ch, stride=ROWS), :] = proj[:ch]
        rsend[i // jr, (i % jr) * ch : (i % jr + 1) * ch, :] = proj[ch:].astype(BF16)
    left = lscr[...].astype(BF16)
    lsend[...] = left
    lbuf[y * nx + x] = left
    rbuf[c, y * NZ + z] = rsend[y]

    pl.semaphore_wait(barrier, peers)

    def send_right(k, carry):
        z2 = lax.rem(z + lax.div(k, ny), NZ)
        y2 = lax.rem(y + lax.rem(k, ny), ny)
        pltpu.make_async_remote_copy(
            rsend.at[y2], rbuf.at[c, y * NZ + z], rsem.at[0], rsem.at[1],
            device_id=device(x, y2, z2, c), device_id_type=MESH,
        ).start()
        return carry

    def send_left(k, carry):
        x2 = lax.rem(x + lax.div(k, ny), nx)
        y2 = lax.rem(y + lax.rem(k, ny), ny)
        pltpu.make_async_remote_copy(
            lsend, lbuf.at[y * nx + x], lsem.at[0], lsem.at[1],
            device_id=device(x2, y2, z, c), device_id_type=MESH,
        ).start()
        return carry

    lax.fori_loop(1, ny * NZ, send_right, 0)
    lax.fori_loop(1, nx * ny, send_left, 0)

    bd[...] = jnp.zeros_like(bd)
    for q in range(ch):
        w = wo_ref[q * ch : (q + 1) * ch, :]
        for t in range(slab):
            bd[(q * slab + t) * ch : (q * slab + t + 1) * ch, t * cz : (t + 1) * cz] = w
    for t, ref in enumerate((ag_ref, ap_ref, bg_ref, bp_ref)):
        wt4[t * cz : (t + 1) * cz, :] = ref[...].astype(F32).T.astype(BF16)

    def many(ref, count, sem):
        part = ref.at[pl.ds(0, count)]
        pltpu.make_async_copy(part, part, sem).wait()

    many(rbuf.at[0], ny * NZ - 1, rsem.at[1])
    cross = pltpu.make_async_remote_copy(
        rbuf.at[c], rbuf.at[c], csem.at[0], csem.at[1], device_id=sibling, device_id_type=MESH
    )
    cross.start()
    many(lbuf, nx * ny - 1, lsem.at[1])

    def outer(half):
        right = rbuf[half]
        right = jnp.concatenate(
            [right[s * NZ : (s + 1) * NZ].reshape(NZ * jr * ch, sd) for s in range(ny)], axis=1
        )

        def one(g, carry):
            rows = jnp.concatenate([lbuf[s * nx + g] for s in range(ny)], axis=1)
            prod = nt(rows, right)
            for q in range(ch):
                part = prod[q * ROWS : (q + 1) * ROWS]
                abuf[half * nx + g, :, q * slab * ch : (q + 1) * slab * ch] = jnp.concatenate(
                    [part[:, t * slab * ch : (t + 1) * slab * ch] for t in range(njo)], axis=0
                ).astype(BF16)
            return carry

        lax.fori_loop(0, nx, one, 0)

    outer(c)
    cross.wait_recv()
    outer(1 - c)
    mixer = abuf[...].reshape(NC * nx * njo * ROWS, slab * ch * ch)
    total = jnp.dot(mixer, bd[...], preferred_element_type=F32)
    step = njo * ROWS
    for h in range(NC):
        for g in range(nx):
            part = total[(h * nx + g) * step : (h * nx + g + 1) * step]
            for t in range(slab):
                tsend[g, h, t] = part[:, t * cz : (t + 1) * cz].astype(BF16)

    for g in range(nx):
        here = jnp.logical_and(x == g, y == x)

        @pl.when(here)
        def _():
            tbuf[y] = tsend[g]

        @pl.when(jnp.logical_not(here))
        def _():
            pltpu.make_async_remote_copy(
                tsend.at[g], tbuf.at[y], tsend_sem.at[g], trecv_sem.at[y],
                device_id=device(g, x, z, c), device_id_type=MESH,
            ).start()

    pair_copy.wait()
    for s in range(ny):

        @pl.when(jnp.logical_not(jnp.logical_and(x == y, y == s)))
        def _():
            pltpu.make_async_copy(tbuf.at[s], tbuf.at[s], trecv_sem.at[s]).wait()

        for h in range(NC):
            for t in range(slab):
                part = tbuf[s, h, t].astype(F32)
                for o in range(njo):
                    flat = o * slab + t
                    j = ((flat // jr) * NC + h) * ROWS + s * jr + flat % jr
                    vbuf[j * ROWS : (j + 1) * ROWS, :] = part[o * ROWS : (o + 1) * ROWS]

    for i in range(ROWS):
        v = pairv[i].astype(F32) + vbuf[pl.ds(i, width, stride=ROWS), :] * (1.0 / seqs)
        u = v.astype(BF16)
        upd[i] = u
        norm = zscore(u.astype(F32), 1).astype(BF16)
        pn[i] = norm
        four = nt(wt4[...], norm)
        lrscr[pl.ds(i, cz, stride=2 * ROWS), :] = jax.nn.sigmoid(four[:cz]) * four[cz : 2 * cz]
        lrscr[pl.ds(ROWS + i, cz, stride=2 * ROWS), :] = (
            jax.nn.sigmoid(four[2 * cz : 3 * cz]) * four[3 * cz :]
        )
    lrsend[...] = lrscr[...].reshape(cz, 2 * ROWS, width).astype(BF16)

    own = y * nxz + x * NZ + z

    def send_channel(k, carry):
        x2, y2, z2 = peer(k)
        pltpu.make_async_remote_copy(
            lrsend.at[y2 * nxz + x2 * NZ + z2], lrbuf.at[own], asem.at[0], asem.at[1],
            device_id=device(x2, y2, z2, c), device_id_type=MESH,
        ).start()
        return carry

    lax.fori_loop(1, peers, send_channel, 0)
    lrbuf[own] = lrsend[own]
    gates[...] = jax.nn.sigmoid(
        jnp.dot(pn[...].reshape(ROWS * width, cz), fg_ref[...], preferred_element_type=F32)
    )
    many(lrbuf, peers - 1, asem.at[1])
    swap = pltpu.make_async_remote_copy(
        lrbuf, lrsib, ssem.at[0], ssem.at[1], device_id=sibling, device_id_type=MESH
    )
    swap.start()

    def wide(ref):
        return jnp.concatenate(
            [ref[s * nxz : (s + 1) * nxz].astype(F32) for s in range(ny)], axis=2
        )

    mine = wide(lrbuf)
    lhs = mine[:, :ROWS].reshape(nxz * ROWS, ny * width).astype(BF16)
    mine = mine[:, ROWS:]
    swap.wait_recv()
    other = wide(lrsib)[:, ROWS:]
    first = c == 0
    rhs = jnp.concatenate([jnp.where(first, mine, other), jnp.where(first, other, mine)], axis=1)
    rhs = rhs.reshape(nxz * NC * ROWS, ny * width).astype(BF16)
    mixed = nt(lhs, rhs)
    for s in range(ny):
        msend[s * nxz : (s + 1) * nxz] = mixed[:, s * width : (s + 1) * width].reshape(
            nxz, ROWS, width
        )

    def send_back(k, carry):
        x2, y2, z2 = peer(k)
        pltpu.make_async_remote_copy(
            msend.at[y2 * nxz + x2 * NZ + z2], mbuf.at[own], msem.at[0], msem.at[1],
            device_id=device(x2, y2, z2, c), device_id_type=MESH,
        ).start()
        return carry

    lax.fori_loop(1, peers, send_back, 0)
    mbuf[own] = msend[own]
    many(mbuf, peers - 1, msem.at[1])

    nscr[...] = zscore(mbuf[...], 0).reshape(cz * ROWS, width)
    for i in range(ROWS):
        norm = nscr[pl.ds(i, cz, stride=ROWS), :].T.astype(BF16)
        proj = jnp.dot(norm, fp_ref[...], preferred_element_type=F32)
        out_ref[i] = (upd[i].astype(F32) + gates[i * width : (i + 1) * width] * proj).astype(BF16)

    many(rbuf.at[0], ny * NZ - 1, rsem.at[0])
    many(lbuf, nx * ny - 1, lsem.at[0])
    cross.wait_send()
    for g in range(nx):

        @pl.when(jnp.logical_not(jnp.logical_and(x == g, y == x)))
        def _():
            pltpu.make_async_copy(tsend.at[g], tsend.at[g], tsend_sem.at[g]).wait()

    many(lrbuf, peers - 1, asem.at[0])
    swap.wait_send()
    many(mbuf, peers - 1, msem.at[0])


def shards(msa, pair, wl, wr, wo, *weights):
    ny = lax.axis_size("blk")
    nx = lax.axis_size("dap") // (NZ * NC)
    sd, _, cm = msa.shape
    ch, cz = wl.shape[1], wo.shape[1]
    jr = ROWS // ny
    width = NZ * NC * ROWS
    step = NZ * jr // 4 * ROWS
    peers = nx * ny * NZ
    vmem = pltpu.VMEM
    scratch = [
        vmem((cm // 128 * sd * ROWS, 128), F32),
        vmem((ch * ROWS, sd), F32),
        vmem((ch * ROWS, sd), BF16),
        vmem((ny * nx, ch * ROWS, sd), BF16),
        vmem((ny, jr * ch, sd), BF16),
        vmem((NC, ny * NZ, jr * ch, sd), BF16),
        vmem((NC * nx, step, 4 * ch * ch), BF16),
        vmem((4 * ch * ch, 4 * cz), BF16),
        vmem((nx, NC, 4, step, cz), BF16),
        vmem((ny, NC, 4, step, cz), BF16),
        vmem((width * ROWS, cz), F32),
        vmem((ROWS, width, cz), BF16),
        vmem((ROWS, width, cz), BF16),
        vmem((ROWS, width, cz), BF16),
        vmem((4 * cz, cz), BF16),
        vmem((cz * 2 * ROWS, width), F32),
        vmem((cz, 2 * ROWS, width), BF16),
        vmem((peers, 2 * ROWS, width), BF16),
        vmem((peers, 2 * ROWS, width), BF16),
        vmem((peers, ROWS, width), F32),
        vmem((peers, ROWS, width), F32),
        vmem((cz * ROWS, width), F32),
        vmem((ROWS * width, cz), F32),
        pltpu.SemaphoreType.DMA,
        pltpu.SemaphoreType.DMA((2,)),
        pltpu.SemaphoreType.DMA((2,)),
        pltpu.SemaphoreType.DMA((2,)),
        pltpu.SemaphoreType.DMA((nx,)),
        pltpu.SemaphoreType.DMA((ny,)),
        pltpu.SemaphoreType.DMA((2,)),
        pltpu.SemaphoreType.DMA((2,)),
        pltpu.SemaphoreType.DMA((2,)),
    ]
    whole = pl.BlockSpec(memory_space=pltpu.VMEM)
    return pl.pallas_call(
        functools.partial(kernel, nx, ny, ny * sd),
        out_shape=jax.ShapeDtypeStruct((ROWS, width, cz), BF16),
        in_specs=[whole, pl.BlockSpec(memory_space=pl.ANY)] + [whole] * 9,
        out_specs=whole,
        scratch_shapes=scratch,
        compiler_params=pltpu.CompilerParams(
            collective_id=0, has_side_effects=True, vmem_limit_bytes=48 * 2**20
        ),
    )(msa.reshape(sd * ROWS, cm), pair, wl, wr, wo, *weights)


def solution(mesh):
    placed = (P("blk", "dap", None), P("dap", None, None)) + (P(),) * 9
    return jax.shard_map(
        shards, mesh=mesh, in_specs=placed, out_specs=P("dap", "blk", None), check_vma=False
    )
```

time: 442 us -> 85.3 us (0.19)
  waiting for transfers between devices: 249 us -> 0 us
  local copies, waits for them, and re-layouts: 100 us -> 6.39 us
  Pallas kernels: 0 us -> 78.5 us
  matrix products: 71.8 us -> 0 us
  between operations: 13.3 us -> 0.08 us
  other arithmetic: 4.75 us -> 0 us
    all_gather x2 -> x0, waiting for transfers between devices: 182 us -> none  [the longest x1 101 us: shards(): lax.all_gather(rhs, 'dap', axis=0, tiled=True)]
    pallas_call x0 -> x1, Pallas kernels: none -> 78.5 us  [shards(): pl.pallas_call(functools.partial(kernel, nx, ny, ny * sd), out_shape=jax....]
    dot_general x25 -> x0, matrix products: 71.8 us -> none  [the longest x8 33.1 us: one_row(): jnp.dot(flat, outer_weight, precision=lax.Precision.HIGHEST, preferred_el...]
    unnamed x20 -> x21, local copies, waits for them, and re-layouts: 60 us -> 6.39 us
    psum x1 -> x0, waiting for transfers between devices: 46.5 us -> none  [shards(): lax.psum(incomplete_accumuland.astype(jnp.bfloat16), 'blk')]
    all_gather x1 -> x0, local copies, waits for them, and re-layouts: 21.5 us -> none  [shards(): lax.all_gather(rhs, 'dap', axis=0, tiled=True)]
    unnamed x5 -> x0, waiting for transfers between devices: 20.1 us -> none
    transpose x8 -> x0, local copies, waits for them, and re-layouts: 9.76 us -> none  [one_row(): jnp.einsum('sc,ser->rce', left_row, piece, preferred_element_type=jnp.flo...]
  transfers between devices with their start and end apart: 4 -> 0, of which waited for: 4 -> 0; matrix products, arithmetic and copies ran while one was open for 1% -> 0% of each run, Pallas kernels for 0% -> 0%
where the time goes in v1:
time: 85.3 us; the launch traced here: 85 us
  Pallas kernels  78.5 us (92%)
  local copies, waits for them, and re-layouts  6.39 us (7%)
    pallas_call x1, Pallas kernels, shards(): pl.pallas_call(functools.partial(kernel, nx, ny, ny * sd), out_shape=jax....  78.5 us
    unnamed x21, local copies, waits for them, and re-layouts  6.39 us

profile of v1, /device:TPU:1, one launch (start us, length us, event | category | flops | bytes accessed | tf_op | source)
XLA Modules:
  0.0 85.0 jit_solution(15866916733782716845)
XLA Ops:
  0.0 0.0 copy-start.5
  0.0 0.0 copy-start.6
  0.0 0.0 copy-start.7
  0.0 0.8 %copy.12.wl_ref = bf16[256,32]{1,0:T(8,128)(2,1)S(1)} copy(bf16[256,32]{0,1:T(8,128)(2,1)} %param.13) | data formatting | bytes 32768 | tf_op args[2]
  0.9 0.0 copy-start.3
  0.9 0.0 copy-start.4
  0.9 0.8 copy.13.wr_ref
  1.7 0.0 copy-done.5
  1.7 0.0 copy-done.6
  1.7 0.0 copy-done.7
  1.8 0.0 copy-done.3
  1.8 0.0 copy-done.4
  1.8 0.0 copy-start
  1.8 1.2 %copy-done = bf16[8,512,128]{2,1,0:T(8,128)(2,1)S(1)} copy-done((bf16[8,512,128]{2,1,0:T(8,128)(2,1)S(1)}, bf16[8,512,128]{2,1,0:T(8,128)(2,1)}, u32[]{:S(2)}) %copy-start) | copy-done | bytes 1048600
  3.0 0.0 copy-start.1
  3.0 1.0 %copy-done.1 = bf16[128,8,256]{2,1,0:T(8,128)(2,1)S(1)} copy-done((bf16[128,8,256]{2,1,0:T(8,128)(2,1)S(1)}, bf16[128,8,256]{2,1,0:T(8,128)(2,1)}, u32[]{:S(2)}) %copy-start.1) | copy-done | bytes 524312
  4.0 0.0 copy-start.2
  4.1 0.9 %copy-done.2 = bf16[1024,128]{1,0:T(8,128)(2,1)S(1)} copy-done((bf16[1024,128]{1,0:T(8,128)(2,1)S(1)}, bf16[1024,128]{1,0:T(8,128)(2,1)}, u32[]{:S(2)}) %copy-start.2) | copy-done | bytes 262168
  5.0 0.0 copy-start.8
  5.0 0.8 copy-done.8
  5.8 78.5 %shard_map.109 = bf16[8,128,128]{2,1,0:T(8,128)(2,1)S(1)} custom-call(bf16[1024,256]{1,0:T(8,128)(2,1)S(1)} %bitcast.1, bf16[8,512,128]{2,1,0:T(8,128)(2,1)S(1)} %copy-done, bf16[256,32]{1,0:T(8,128)(2,1)S(1)} %copy.12.wl_ref, bf16[256,32]{1,0:T(8,128)(2,1)S(1)} %copy.13.wr_ref, bf16[1024,128]{1,0:T(8,128)(2,1)S(1)} %copy-done.2, ...), custom_call_target="tpu_custom_call" | custom-call | tf_op jit(solution)/shard_map/pallas_call | solution.py:325
  84.3 0.7 copy.15
Async XLA Ops:
  0.0 1.7 %copy-start.5 = (bf16[128,128]{1,0:T(8,128)(2,1)S(1)}, bf16[128,128]{1,0:T(8,128)(2,1)}, u32[]{:S(2)}) copy-start(bf16[128,128]{1,0:T(8,128)(2,1)} %bg_ref.1) | copy-start | bytes 98308
  0.0 1.7 %copy-start.6 = (bf16[128,128]{1,0:T(8,128)(2,1)S(1)}, bf16[128,128]{1,0:T(8,128)(2,1)}, u32[]{:S(2)}) copy-start(bf16[128,128]{1,0:T(8,128)(2,1)} %bp_ref.1) | copy-start | bytes 98308
  0.0 1.7 %copy-start.7 = (bf16[128,128]{1,0:T(8,128)(2,1)S(1)}, bf16[128,128]{1,0:T(8,128)(2,1)}, u32[]{:S(2)}) copy-start(bf16[128,128]{1,0:T(8,128)(2,1)} %fg_ref.1) | copy-start | bytes 98308
  0.9 0.9 %copy-start.3 = (bf16[128,128]{1,0:T(8,128)(2,1)S(1)}, bf16[128,128]{1,0:T(8,128)(2,1)}, u32[]{:S(2)}) copy-start(bf16[128,128]{1,0:T(8,128)(2,1)} %ag_ref.1) | copy-start | bytes 98308
  0.9 0.9 %copy-start.4 = (bf16[128,128]{1,0:T(8,128)(2,1)S(1)}, bf16[128,128]{1,0:T(8,128)(2,1)}, u32[]{:S(2)}) copy-start(bf16[128,128]{1,0:T(8,128)(2,1)} %ap_ref.1) | copy-start | bytes 98308
  1.8 1.2 %copy-start = (bf16[8,512,128]{2,1,0:T(8,128)(2,1)S(1)}, bf16[8,512,128]{2,1,0:T(8,128)(2,1)}, u32[]{:S(2)}) copy-start(bf16[8,512,128]{2,1,0:T(8,128)(2,1)} %pair_ref.1) | copy-start | bytes 3145732
  3.0 1.0 %copy-start.1 = (bf16[128,8,256]{2,1,0:T(8,128)(2,1)S(1)}, bf16[128,8,256]{2,1,0:T(8,128)(2,1)}, u32[]{:S(2)}) copy-start(bf16[128,8,256]{2,1,0:T(8,128)(2,1)} %param.11) | copy-start | bytes 1572868
  4.0 0.9 %copy-start.2 = (bf16[1024,128]{1,0:T(8,128)(2,1)S(1)}, bf16[1024,128]{1,0:T(8,128)(2,1)}, u32[]{:S(2)}) copy-start(bf16[1024,128]{1,0:T(8,128)(2,1)} %wo_ref.1) | copy-start | bytes 786436
  5.0 0.8 copy-start.8

commit v2 on v1

--- a/solution.py
+++ b/solution.py
@@ -36,13 +36,15 @@
     out_ref,
     xf, lscr, lsend, lbuf, rsend, rbuf, abuf, bd, tsend, tbuf, vbuf, pairv, upd, pn, wt4,
     lrscr, lrsend, lrbuf, lrsib, msend, mbuf, nscr, gates,
-    pair_sem, lsem, rsem, csem, tsend_sem, trecv_sem, asem, ssem, msem,
+    msa_v, wl_v, wr_v, wo_v, ag_v, ap_v, bg_v, bp_v, fg_v, fp_v,
+    load_sem, pair_sem, lsem, rsem, csem, tsend_sem, trecv_sem, asem, ssem, msem,
 ):
+    local = (msa_v, wl_v, wr_v, wo_v, ag_v, ap_v, bg_v, bp_v, fg_v, fp_v)
     d = lax.axis_index("dap")
     y = lax.axis_index("blk")
     x, z, c = d // (NZ * NC), (d // NC) % NZ, d % NC
     sd = msa_ref.shape[0] // ROWS
-    ch = wl_ref.shape[1]
+    ch = wl_ref.shape[0]
     cz = wo_ref.shape[1]
     jr = ROWS // ny
     slab = 4
@@ -59,25 +61,43 @@
         y2 = lax.rem(y + lax.rem(r, ny), ny)
         return x2, y2, z2
 
-    def greet(k, carry):
-        x2, y2, z2 = peer(k)
-        pl.semaphore_signal(barrier, inc=1, device_id=device(x2, y2, z2, c), device_id_type=MESH)
-        return carry
-
     barrier = pltpu.get_barrier_semaphore()
-    pl.semaphore_signal(barrier, inc=1, device_id=sibling, device_id_type=MESH)
-    lax.fori_loop(1, peers, greet, 0)
-
+
+    def greet(x2, y2, z2, c2):
+        pl.semaphore_signal(barrier, inc=1, device_id=device(x2, y2, z2, c2), device_id_type=MESH)
+
+    def greet_yz(k, carry):
+        greet(x, lax.rem(y + lax.rem(k, ny), ny), lax.rem(z + lax.div(k, ny), NZ), c)
+        return carry
+
+    def greet_xy(k, carry):
+        greet(lax.rem(x + lax.div(k, ny), nx), lax.rem(y + lax.rem(k, ny), ny), z, c)
+        return carry
+
+    greet(x, y, z, 1 - c)
+    lax.fori_loop(1, ny * NZ, greet_yz, 0)
+    lax.fori_loop(ny, nx * ny, greet_xy, 0)
+
+    sources = (msa_ref, wl_ref, wr_ref, wo_ref, ag_ref, ap_ref, bg_ref, bp_ref, fg_ref, fp_ref)
+    loads = [
+        pltpu.make_async_copy(source, target, load_sem.at[t])
+        for t, (source, target) in enumerate(zip(sources, local))
+    ]
+    for load in loads:
+        load.start()
+    msa_ref, wl_ref, wr_ref, wo_ref, ag_ref, ap_ref, bg_ref, bp_ref, fg_ref, fp_ref = local
     pair_copy = pltpu.make_async_copy(
         pair_ref.at[:, pl.ds(pl.multiple_of(y * width, width), width), :], pairv, pair_sem
     )
     pair_copy.start()
+    for load in loads[:3]:
+        load.wait()
 
     lanes = xf.shape[1]
     blocks = msa_ref.shape[1] // lanes
     for h in range(blocks):
         xf[h * sd * ROWS : (h + 1) * sd * ROWS] = msa_ref[:, h * lanes : (h + 1) * lanes].astype(F32)
-    wlr = jnp.concatenate([wl_ref[...].astype(F32).T, wr_ref[...].astype(F32).T], axis=0).astype(BF16)
+    wlr = jnp.concatenate([wl_ref[...], wr_ref[...]], axis=0)
     for i in range(ROWS):
         v = jnp.concatenate(
             [xf[pl.ds(h * sd * ROWS + i, sd, stride=ROWS), :] for h in range(blocks)], axis=1
@@ -91,7 +111,7 @@
     lbuf[y * nx + x] = left
     rbuf[c, y * NZ + z] = rsend[y]
 
-    pl.semaphore_wait(barrier, peers)
+    pl.semaphore_wait(barrier, ny * NZ + (nx - 1) * ny)
 
     def send_right(k, carry):
         z2 = lax.rem(z + lax.div(k, ny), NZ)
@@ -114,6 +134,8 @@
     lax.fori_loop(1, ny * NZ, send_right, 0)
     lax.fori_loop(1, nx * ny, send_left, 0)
 
+    for load in loads[3:]:
+        load.wait()
     bd[...] = jnp.zeros_like(bd)
     for q in range(ch):
         w = wo_ref[q * ch : (q + 1) * ch, :]
@@ -311,6 +333,12 @@
         vmem((peers, ROWS, width), F32),
         vmem((cz * ROWS, width), F32),
         vmem((ROWS * width, cz), F32),
+        vmem((sd * ROWS, cm), BF16),
+        vmem((ch, cm), BF16),
+        vmem((ch, cm), BF16),
+        vmem((ch * ch, cz), BF16),
+    ] + [vmem((cz, cz), BF16)] * 6 + [
+        pltpu.SemaphoreType.DMA((10,)),
         pltpu.SemaphoreType.DMA,
         pltpu.SemaphoreType.DMA((2,)),
         pltpu.SemaphoreType.DMA((2,)),
@@ -321,17 +349,16 @@
         pltpu.SemaphoreType.DMA((2,)),
         pltpu.SemaphoreType.DMA((2,)),
     ]
-    whole = pl.BlockSpec(memory_space=pltpu.VMEM)
     return pl.pallas_call(
         functools.partial(kernel, nx, ny, ny * sd),
         out_shape=jax.ShapeDtypeStruct((ROWS, width, cz), BF16),
-        in_specs=[whole, pl.BlockSpec(memory_space=pl.ANY)] + [whole] * 9,
-        out_specs=whole,
+        in_specs=[pl.BlockSpec(memory_space=pltpu.HBM)] * 11,
+        out_specs=pl.BlockSpec(memory_space=pltpu.VMEM),
         scratch_shapes=scratch,
         compiler_params=pltpu.CompilerParams(
-            collective_id=0, has_side_effects=True, vmem_limit_bytes=48 * 2**20
+            collective_id=0, has_side_effects=True, vmem_limit_bytes=60 * 2**20
         ),
-    )(msa.reshape(sd * ROWS, cm), pair, wl, wr, wo, *weights)
+    )(msa.reshape(sd * ROWS, cm), pair, wl.T, wr.T, wo, *weights)
 
 
 def solution(mesh):

time: 85.3 us -> 77.6 us (0.910)
  local copies, waits for them, and re-layouts: 6.39 us -> 1.67 us
  Pallas kernels: 78.5 us -> 75.8 us
    unnamed x21 -> x1, local copies, waits for them, and re-layouts: 6.39 us -> 1.67 us
    pallas_call x1, Pallas kernels: 78.5 us -> 75.8 us  [shards(): pl.pallas_call(functools.partial(kernel, nx, ny, ny * sd), out_shape=jax....]
where the time goes in v2:
time: 77.6 us; the launch traced here: 77.5 us
  Pallas kernels  75.8 us (98%)
  local copies, waits for them, and re-layouts  1.67 us (2%)
    pallas_call x1, Pallas kernels, shards(): pl.pallas_call(functools.partial(kernel, nx, ny, ny * sd), out_shape=jax....  75.8 us
    unnamed x1, local copies, waits for them, and re-layouts  1.67 us

profile of v2, /device:TPU:1, one launch (start us, length us, event | category | flops | bytes accessed | tf_op | source)
XLA Modules:
  0.0 77.5 jit_solution(13415592123796035615)
XLA Ops:
  0.0 75.8 %shard_map.109 = bf16[8,128,128]{2,1,0:T(8,128)(2,1)} custom-call(bf16[1024,256]{1,0:T(8,128)(2,1)} %bitcast.3, bf16[8,512,128]{2,1,0:T(8,128)(2,1)} %pair_ref.1, bf16[32,256]{1,0:T(8,128)(2,1)} %bitcast.4, bf16[32,256]{1,0:T(8,128)(2,1)} %bitcast.5, bf16[1024,128]{1,0:T(8,128)(2,1)} %wo_ref.1, bf16[128,128]{1,0:T(8,128)(2,1)} %ag_ref.1, ...), custom_call_target="tpu_custom_call" | custom-call | tf_op jit(solution)/shard_map/pallas_call | solution.py:352
  75.8 1.7 %copy.13 = bf16[8,128,128]{2,1,0:T(8,128)(2,1)} copy(bf16[8,128,128]{2,1,0:T(8,128)(2,1)} %shard_map.109) | data formatting | bytes 524288

commit v3 on v2

v3 whole, which is shorter than its diff:
```python
import functools

import jax
import jax.numpy as jnp
from jax import lax
from jax.experimental import pallas as pl
from jax.experimental.pallas import tpu as pltpu
from jax.sharding import PartitionSpec as P

NZ = 8
NC = 2
ROWS = 8
EPS = 1e-5
MESH = pl.DeviceIdType.MESH
F32 = jnp.float32
BF16 = jnp.bfloat16


def nt(a, b):
    return lax.dot_general(a, b, (((1,), (1,)), ((), ())), preferred_element_type=F32)


def zscore(v, axis):
    centered = v - jnp.mean(v, axis=axis, keepdims=True)
    var = jnp.mean(centered * centered, axis=axis, keepdims=True)
    return centered * lax.rsqrt(var + EPS)


def device(x, y, z, c):
    return (x * NZ + z) * NC + c, y


def kernel(
    nx, ny, seqs,
    msa_ref, pair_ref, wl_ref, wr_ref, wo_ref, ag_ref, ap_ref, bg_ref, bp_ref, fg_ref, fp_ref,
    out_ref,
    xf, lscr, lbuf, rsend, rbuf, abuf, bd, pairv, pairf, pstage, psend, pbuf, usend, ubuf, vbuf, upd,
    wt4, lrscr, lrsend, lrbuf, lrsib, lwide, rwide, msend, mbuf, nscr, gates,
    msa_v, wl_v, wr_v, wo_v, ag_v, ap_v, bg_v, bp_v, fg_v, fp_v,
    load_sem, pair_sem, lsem, rsem, csem, psem, usend_sem, urecv_sem, asem, ssem, msem, fsem,
):
    local = (msa_v, wl_v, wr_v, wo_v, ag_v, ap_v, bg_v, bp_v, fg_v, fp_v)
    d = lax.axis_index("dap")
    y = lax.axis_index("blk")
    x, z, c = d // (NZ * NC), (d // NC) % NZ, d % NC
    sd = msa_ref.shape[0] // ROWS
    ch = wl_ref.shape[0]
    cz = wo_ref.shape[1]
    jr = ROWS // ny
    slab = 4
    njo = NZ * jr // slab
    thirds = NC * NZ * jr
    width = NZ * NC * ROWS
    nyx = ny * nx
    zh = NZ // 2
    peers = nyx * NZ
    sibling = device(x, y, z, 1 - c)
    first = c == 0

    def place(x1, y1, z1):
        return (y1 * nx + x1) * NZ + lax.rem(z1, 2) * zh + lax.div(z1, 2)

    def remote(source, target, send, recv, to):
        return pltpu.make_async_remote_copy(
            source, target, send, recv, device_id=to, device_id_type=MESH
        )

    def arrived(part, sem):
        pltpu.make_async_copy(part, part, sem).wait()

    barrier = pltpu.get_barrier_semaphore()

    def greet(x2, y2, z2, c2):
        pl.semaphore_signal(barrier, inc=1, device_id=device(x2, y2, z2, c2), device_id_type=MESH)

    def greet_yz(k, carry):
        greet(x, lax.rem(y + lax.rem(k, ny), ny), lax.rem(z + lax.div(k, ny), NZ), c)
        return carry

    greet(x, y, z, 1 - c)
    for k in range(1, nx):
        greet(lax.rem(x + k, nx), y, z, c)
    lax.fori_loop(1, ny * NZ, greet_yz, 0)

    sources = (msa_ref, wl_ref, wr_ref, wo_ref, ag_ref, ap_ref, bg_ref, bp_ref, fg_ref, fp_ref)
    loads = [
        pltpu.make_async_copy(source, target, load_sem.at[t])
        for t, (source, target) in enumerate(zip(sources, local))
    ]
    for load in loads:
        load.start()
    pair_copy = pltpu.make_async_copy(pair_ref, pairv, pair_sem)
    pair_copy.start()
    for load in loads[:3]:
        load.wait()

    lanes = xf.shape[1]
    blocks = msa_v.shape[1] // lanes
    for h in range(blocks):
        xf[h * sd * ROWS : (h + 1) * sd * ROWS] = msa_v[:, h * lanes : (h + 1) * lanes].astype(F32)
    wlr = jnp.concatenate([wl_v[...], wr_v[...]], axis=0)
    for i in range(ROWS):
        v = jnp.concatenate(
            [xf[pl.ds(h * sd * ROWS + i, sd, stride=ROWS), :] for h in range(blocks)], axis=1
        )
        v = zscore(v, 1).astype(BF16)
        proj = nt(wlr, v)
        lscr[pl.ds(i, ch, stride=ROWS), :] = proj[:ch]
        rsend[i // jr, (i % jr) * ch : (i % jr + 1) * ch, :] = proj[ch:].astype(BF16)
    lbuf[y, x] = lscr[...].astype(BF16)
    rbuf[c, y * NZ + z] = rsend[y]

    pl.semaphore_wait(barrier, ny * NZ + nx - 1)

    half = ch * ROWS // 2
    low, high = pl.ds(0, half), pl.ds(half, half)
    xfirst = lbuf.at[y, x, low]
    yfirst = lbuf.at[y, x, high]
    for k in range(1, nx):
        remote(xfirst, xfirst, lsem.at[0], lsem.at[1], device(lax.rem(x + k, nx), y, z, c)).start()
    for k in range(1, ny):
        remote(yfirst, yfirst, lsem.at[2], lsem.at[3], device(x, lax.rem(y + k, ny), z, c)).start()

    def send_right(k, carry):
        z2 = lax.rem(z + lax.div(k, ny), NZ)
        y2 = lax.rem(y + lax.rem(k, ny), ny)
        remote(
            rsend.at[y2], rbuf.at[c, y * NZ + z], rsem.at[0], rsem.at[1], device(x, y2, z2, c)
        ).start()
        return carry

    lax.fori_loop(1, ny * NZ, send_right, 0)

    arrived(lbuf.at[0, pl.ds(0, nx - 1), low], lsem.at[1])
    ythen = lbuf.at[y, :, low]
    for k in range(1, ny):
        remote(ythen, ythen, lsem.at[4], lsem.at[5], device(x, lax.rem(y + k, ny), z, c)).start()
    arrived(lbuf.at[pl.ds(0, ny - 1), 0, high], lsem.at[3])
    xthen = lbuf.at[:, x, high]
    for k in range(1, nx):
        remote(xthen, xthen, lsem.at[6], lsem.at[7], device(lax.rem(x + k, nx), y, z, c)).start()

    pair_copy.wait()
    columns = pairv.shape[1]
    pairf[...] = pairv[...].astype(F32).reshape(ROWS * columns, cz)
    for i in range(ROWS):
        for h in range(NC):
            for r in range(jr):
                v = pairf[pl.ds(i * columns + h * ROWS + y * jr + r, nx * NZ, stride=NC * ROWS), :]
                for g in range(nx):
                    start = (g * thirds + h * NZ * jr + r) * ROWS + i
                    pstage[pl.ds(start, NZ, stride=jr * ROWS), :] = v[g * NZ : (g + 1) * NZ]
    psend[...] = pstage[...].astype(BF16).reshape(nx, thirds * ROWS, cz)
    pbuf[x] = psend[x]
    for k in range(1, nx):
        x2 = lax.rem(x + k, nx)
        remote(psend.at[x2], pbuf.at[x], psem.at[0], psem.at[1], device(x2, y, z, c)).start()

    for load in loads[3:]:
        load.wait()
    bd[...] = jnp.zeros_like(bd)
    for q in range(ch):
        w = wo_v[q * ch : (q + 1) * ch, :]
        for t in range(slab):
            bd[(q * slab + t) * ch : (q * slab + t + 1) * ch, t * cz : (t + 1) * cz] = w
    for t, ref in enumerate((ag_v, ap_v, bg_v, bp_v)):
        wt4[t * cz : (t + 1) * cz, :] = ref[...].astype(F32).T.astype(BF16)

    arrived(rbuf.at[0, pl.ds(0, ny * NZ - 1)], rsem.at[1])
    cross = remote(rbuf.at[c], rbuf.at[c], csem.at[0], csem.at[1], sibling)
    cross.start()
    arrived(lbuf.at[pl.ds(0, ny - 1), :, low], lsem.at[5])
    arrived(lbuf.at[:, pl.ds(0, nx - 1), high], lsem.at[7])

    def outer(side):
        right = rbuf[side]
        right = jnp.concatenate(
            [right[s * NZ : (s + 1) * NZ].reshape(NZ * jr * ch, sd) for s in range(ny)], axis=1
        )

        def one(g, carry):
            rows = jnp.concatenate([lbuf[s, g] for s in range(ny)], axis=1)
            prod = nt(rows, right)
            for q in range(ch):
                part = prod[q * ROWS : (q + 1) * ROWS]
                abuf[side * nx + g, :, q * slab * ch : (q + 1) * slab * ch] = jnp.concatenate(
                    [part[:, t * slab * ch : (t + 1) * slab * ch] for t in range(njo)], axis=0
                ).astype(BF16)
            return carry

        lax.fori_loop(0, nx, one, 0)

    outer(c)
    cross.wait_recv()
    outer(1 - c)
    step = njo * ROWS
    mixer = abuf[...].reshape(NC * nx * step, slab * ch * ch)
    total = jnp.dot(mixer, bd[...], preferred_element_type=F32)

    arrived(pbuf.at[pl.ds(0, nx - 1)], psem.at[1])
    for g in range(nx):
        tiles = []
        for kk in range(thirds):
            h, flat = divmod(kk, NZ * jr)
            o, t = divmod(flat, slab)
            start = (h * nx + g) * step + o * ROWS
            tiles.append(total[start : start + ROWS, t * cz : (t + 1) * cz])
        u = pbuf[g].astype(F32) + jnp.concatenate(tiles, axis=0) * (1.0 / seqs)
        u = u.astype(BF16)
        usend[g] = u
        vbuf[g * thirds * ROWS : (g + 1) * thirds * ROWS] = u.astype(F32)

    for i in range(ROWS):
        norm = zscore(vbuf[pl.ds(i, width, stride=ROWS), :], 1).astype(BF16)
        four = nt(wt4[...], norm)
        lrscr[pl.ds(i, cz, stride=2 * ROWS), :] = jax.nn.sigmoid(four[:cz]) * four[cz : 2 * cz]
        lrscr[pl.ds(ROWS + i, cz, stride=2 * ROWS), :] = (
            jax.nn.sigmoid(four[2 * cz : 3 * cz]) * four[3 * cz :]
        )
    lrsend[...] = lrscr[...].reshape(cz, 2 * ROWS, width).astype(BF16)

    own = place(x, y, z)

    def send_channel(k, carry):
        r = lax.rem(k, ny * NZ)
        x2 = lax.rem(x + lax.div(k, ny * NZ), nx)
        z2 = lax.rem(z + lax.div(r, ny), NZ)
        y2 = lax.rem(y + lax.rem(r, ny), ny)
        remote(
            lrsend.at[place(x2, y2, z2)], lrbuf.at[own], asem.at[0], asem.at[1],
            device(x2, y2, z2, c),
        ).start()
        return carry

    lax.fori_loop(1, peers, send_channel, 0)
    lrbuf[own] = lrsend[own]

    for g in range(nx):
        here = jnp.logical_and(x == g, y == x)

        @pl.when(here)
        def _():
            ubuf[y] = usend[g]

        @pl.when(jnp.logical_not(here))
        def _():
            remote(
                usend.at[g], ubuf.at[y], usend_sem.at[g], urecv_sem.at[y], device(g, x, z, c)
            ).start()

    for s in range(ny):

        @pl.when(jnp.logical_not(jnp.logical_and(x == y, y == s)))
        def _():
            arrived(ubuf.at[s], urecv_sem.at[s])

        part = ubuf[s].astype(F32)
        for kk in range(thirds):
            h, flat = divmod(kk, NZ * jr)
            j = ((flat // jr) * NC + h) * ROWS + s * jr + flat % jr
            vbuf[j * ROWS : (j + 1) * ROWS, :] = part[kk * ROWS : (kk + 1) * ROWS]
    for i in range(ROWS):
        u = vbuf[pl.ds(i, width, stride=ROWS), :]
        upd[i] = u
        norm = zscore(u, 1).astype(BF16)
        gates[i] = jax.nn.sigmoid(jnp.dot(norm, fg_v[...], preferred_element_type=F32))

    arrived(lrbuf.at[pl.ds(0, peers - 1)], asem.at[1])
    swaps = []
    for s in range(ny):
        part = pl.ds(s * nx * NZ, nx * NZ)
        swaps.append(remote(lrbuf.at[part], lrsib.at[part], ssem.at[0, s], ssem.at[1, s], sibling))
        swaps[-1].start()
    group = lax.broadcasted_iota(jnp.int32, (zh * NC * ROWS, width), 1) // thirds
    for s in range(nyx):
        if s % nx == 0:
            swaps[s // nx].wait_recv()
        mine = lrbuf[s * NZ : (s + 1) * NZ].astype(F32)
        other = lrsib[s * NZ : (s + 1) * NZ].astype(F32)
        m0, m1 = jnp.where(first, mine, other), jnp.where(first, other, mine)
        span = slice(s * width, (s + 1) * width)
        rows = []
        for z2 in range(NZ):
            at = z2 % 2 * zh + z2 // 2
            rows += [m0[at, ROWS:], m1[at, ROWS:]]
        right = jnp.concatenate(rows, axis=0)
        for m in range(nx):
            rolled = pltpu.roll(right, m * thirds, 1) if m else right
            rwide[m * width : (m + 1) * width, span] = rolled.astype(BF16)
        rows = []
        for m in (m0, m1):
            rows.append(jnp.where(first, m[:zh, :ROWS], m[zh:, :ROWS]))
        left = jnp.concatenate(rows, axis=1).reshape(zh * NC * ROWS, width)
        for g in range(nx):
            lwide[g * zh * NC * ROWS : (g + 1) * zh * NC * ROWS, span] = jnp.where(
                group == g, left, 0.0
            ).astype(BF16)
    mixed = nt(lwide[...], rwide[...])
    for g in range(nx):
        for m in range(nx):
            g2 = (g - m) % nx
            part = mixed[g * zh * NC * ROWS : (g + 1) * zh * NC * ROWS, m * width : (m + 1) * width]
            msend[(g2 * nx + g) * zh : (g2 * nx + g + 1) * zh] = part.reshape(
                zh, NC * ROWS, width
            ).astype(BF16)

    side = lax.rem(z, 2)
    home = (y * nx + x) * zh + lax.div(z, 2)

    def send_back(k, carry):
        x2 = lax.rem(x + lax.div(k, ny * zh), nx)
        y2 = lax.rem(y + lax.rem(lax.div(k, zh), ny), ny)
        zh2 = lax.rem(lax.div(z, 2) + lax.rem(k, zh), zh)
        remote(
            msend.at[(y2 * nx + x2) * zh + zh2], mbuf.at[side, home], msem.at[0], msem.at[1],
            device(x2, y2, 2 * zh2 + c, side),
        ).start()
        return carry

    stays = side == c
    lax.fori_loop(1, nyx * zh, send_back, 0)

    @pl.when(stays)
    def _():
        mbuf[side, home] = msend[home]
        arrived(mbuf.at[c, pl.ds(0, nyx * zh - 1)], msem.at[1])

    @pl.when(jnp.logical_not(stays))
    def _():
        send_back(0, 0)
        arrived(mbuf.at[c], msem.at[1])

    final = remote(mbuf.at[c], mbuf.at[c], fsem.at[0], fsem.at[1], sibling)
    final.start()
    final.wait_recv()

    full = mbuf[...].astype(F32)
    full = jnp.where(first, full[:, :, :ROWS], full[:, :, ROWS:])
    norm = zscore(full.reshape(cz, ROWS, width), 0)
    for p in range(2):
        for s in range(nyx):
            start = s * NZ + p * zh
            part = norm[(p * nyx + s) * zh : (p * nyx + s + 1) * zh]
            nscr[start * ROWS : (start + zh) * ROWS] = part.reshape(zh * ROWS, width)
    for i in range(ROWS):
        norm = nscr[pl.ds(i, cz, stride=ROWS), :].T.astype(BF16)
        proj = jnp.dot(norm, fp_v[...], preferred_element_type=F32)
        out_ref[i] = (upd[i] + gates[i] * proj).astype(BF16)

    arrived(lbuf.at[0, pl.ds(0, nx - 1), low], lsem.at[0])
    arrived(lbuf.at[pl.ds(0, ny - 1), 0, high], lsem.at[2])
    arrived(lbuf.at[pl.ds(0, ny - 1), :, low], lsem.at[4])
    arrived(lbuf.at[:, pl.ds(0, nx - 1), high], lsem.at[6])
    arrived(rbuf.at[0, pl.ds(0, ny * NZ - 1)], rsem.at[0])
    arrived(psend.at[pl.ds(0, nx - 1)], psem.at[0])
    cross.wait_send()
    for g in range(nx):

        @pl.when(jnp.logical_not(jnp.logical_and(x == g, y == x)))
        def _():
            arrived(usend.at[g], usend_sem.at[g])

    arrived(lrbuf.at[pl.ds(0, peers - 1)], asem.at[0])
    for swap in swaps:
        swap.wait_send()

    @pl.when(stays)
    def _():
        arrived(msend.at[pl.ds(0, nyx * zh - 1)], msem.at[0])

    @pl.when(jnp.logical_not(stays))
    def _():
        arrived(msend, msem.at[0])

    final.wait_send()


def shards(msa, pair, wl, wr, wo, *weights):
    ny = lax.axis_size("blk")
    nx = lax.axis_size("dap") // (NZ * NC)
    sd, _, cm = msa.shape
    ch, cz = wl.shape[1], wo.shape[1]
    columns = pair.shape[1]
    jr = ROWS // ny
    width = NZ * NC * ROWS
    thirds = NC * NZ * jr
    step = NZ * jr // 4 * ROWS
    peers = nx * ny * NZ
    vmem = pltpu.VMEM
    dma = pltpu.SemaphoreType.DMA
    scratch = [
        vmem((cm // 128 * sd * ROWS, 128), F32),
        vmem((ch * ROWS, sd), F32),
        vmem((ny, nx, ch * ROWS, sd), BF16),
        vmem((ny, jr * ch, sd), BF16),
        vmem((NC, ny * NZ, jr * ch, sd), BF16),
        vmem((NC * nx, step, 4 * ch * ch), BF16),
        vmem((4 * ch * ch, 4 * cz), BF16),
        vmem((ROWS, columns, cz), BF16),
        vmem((ROWS * columns, cz), F32),
        vmem((nx * thirds * ROWS, cz), F32),
        vmem((nx, thirds * ROWS, cz), BF16),
        vmem((nx, thirds * ROWS, cz), BF16),
        vmem((nx, thirds * ROWS, cz), BF16),
        vmem((ny, thirds * ROWS, cz), BF16),
        vmem((width * ROWS, cz), F32),
        vmem((ROWS, width, cz), F32),
        vmem((4 * cz, cz), BF16),
        vmem((cz * 2 * ROWS, width), F32),
        vmem((cz, 2 * ROWS, width), BF16),
        vmem((peers, 2 * ROWS, width), BF16),
        vmem((peers, 2 * ROWS, width), BF16),
        vmem((nx * NZ * ROWS, ny * nx * width), BF16),
        vmem((nx * width, ny * nx * width), BF16),
        vmem((peers // 2, 2 * ROWS, width), BF16),
        vmem((2, peers // 2, 2 * ROWS, width), BF16),
        vmem((cz * ROWS, width), F32),
        vmem((ROWS, width, cz), F32),
        vmem((sd * ROWS, cm), BF16),
        vmem((ch, cm), BF16),
        vmem((ch, cm), BF16),
        vmem((ch * ch, cz), BF16),
    ] + [vmem((cz, cz), BF16)] * 6 + [
        dma((10,)),
        dma,
        dma((8,)),
        dma((2,)),
        dma((2,)),
        dma((2,)),
        dma((nx,)),
        dma((ny,)),
        dma((2,)),
        dma((2, ny)),
        dma((2,)),
        dma((2,)),
    ]
    return pl.pallas_call(
        functools.partial(kernel, nx, ny, ny * sd),
        out_shape=jax.ShapeDtypeStruct((ROWS, width, cz), BF16),
        in_specs=[pl.BlockSpec(memory_space=pltpu.HBM)] * 11,
        out_specs=pl.BlockSpec(memory_space=pltpu.VMEM),
        scratch_shapes=scratch,
        compiler_params=pltpu.CompilerParams(
            collective_id=0, has_side_effects=True, vmem_limit_bytes=60 * 2**20
        ),
    )(msa.reshape(sd * ROWS, cm), pair, wl.T, wr.T, wo, *weights)


def solution(mesh):
    placed = (P("blk", "dap", None), P("dap", None, None)) + (P(),) * 9
    return jax.shard_map(
        shards, mesh=mesh, in_specs=placed, out_specs=P("dap", "blk", None), check_vma=False
    )
```

time: 77.6 us -> 66.3 us (0.85)
  Pallas kernels: 75.8 us -> 64.5 us
    pallas_call x1, Pallas kernels: 75.8 us -> 64.5 us  [shards(): pl.pallas_call(functools.partial(kernel, nx, ny, ny * sd), out_shape=jax....]
where the time goes in v3:
time: 66.3 us; the launch traced here: 66.2 us
  Pallas kernels  64.5 us (97%)
  local copies, waits for them, and re-layouts  1.67 us (3%)
    pallas_call x1, Pallas kernels, shards(): pl.pallas_call(functools.partial(kernel, nx, ny, ny * sd), out_shape=jax....  64.5 us
    unnamed x1, local copies, waits for them, and re-layouts  1.67 us

profile of v3, /device:TPU:1, one launch (start us, length us, event | category | flops | bytes accessed | tf_op | source)
XLA Modules:
  0.0 66.2 jit_solution(16676038259994415043)
XLA Ops:
  0.0 64.5 %shard_map.109 = bf16[8,128,128]{2,1,0:T(8,128)(2,1)} custom-call(bf16[1024,256]{1,0:T(8,128)(2,1)} %bitcast.3, bf16[8,512,128]{2,1,0:T(8,128)(2,1)} %pair_ref.1, bf16[32,256]{1,0:T(8,128)(2,1)} %bitcast.4, bf16[32,256]{1,0:T(8,128)(2,1)} %bitcast.5, bf16[1024,128]{1,0:T(8,128)(2,1)} %wo_ref.1, bf16[128,128]{1,0:T(8,128)(2,1)} %ag_ref.1, ...), custom_call_target="tpu_custom_call" | custom-call | tf_op jit(solution)/shard_map/pallas_call | solution.py:437
  64.6 1.7 %copy.13 = bf16[8,128,128]{2,1,0:T(8,128)(2,1)} copy(bf16[8,128,128]{2,1,0:T(8,128)(2,1)} %shard_map.109) | data formatting | bytes 524288

commit v4 on v3

--- a/solution.py
+++ b/solution.py
@@ -35,7 +35,7 @@
     msa_ref, pair_ref, wl_ref, wr_ref, wo_ref, ag_ref, ap_ref, bg_ref, bp_ref, fg_ref, fp_ref,
     out_ref,
     xf, lscr, lbuf, rsend, rbuf, abuf, bd, pairv, pairf, pstage, psend, pbuf, usend, ubuf, vbuf, upd,
-    wt4, lrscr, lrsend, lrbuf, lrsib, lwide, rwide, msend, mbuf, nscr, gates,
+    wt4, lrscr, lrsend, lrbuf, lrsib, lwide, rwide, mixed, msend, mbuf, nscr, gates,
     msa_v, wl_v, wr_v, wo_v, ag_v, ap_v, bg_v, bp_v, fg_v, fp_v,
     load_sem, pair_sem, lsem, rsem, csem, psem, usend_sem, urecv_sem, asem, ssem, msem, fsem,
 ):
@@ -53,17 +53,19 @@
     width = NZ * NC * ROWS
     nyx = ny * nx
     zh = NZ // 2
-    peers = nyx * NZ
     sibling = device(x, y, z, 1 - c)
     first = c == 0
 
     def place(x1, y1, z1):
-        return (y1 * nx + x1) * NZ + lax.rem(z1, 2) * zh + lax.div(z1, 2)
+        return (x1 * ny + y1) * NZ + lax.rem(z1, 2) * zh + lax.div(z1, 2)
 
     def remote(source, target, send, recv, to):
         return pltpu.make_async_remote_copy(
             source, target, send, recv, device_id=to, device_id_type=MESH
         )
+
+    def away(k, n):
+        return lax.rem(n // 2 + jnp.where(lax.rem(k, 2) == 1, lax.div(k + 1, 2), n - lax.div(k, 2)), n)
 
     def arrived(part, sem):
         pltpu.make_async_copy(part, part, sem).wait()
@@ -221,18 +223,24 @@
 
     own = place(x, y, z)
 
-    def send_channel(k, carry):
-        r = lax.rem(k, ny * NZ)
-        x2 = lax.rem(x + lax.div(k, ny * NZ), nx)
-        z2 = lax.rem(z + lax.div(r, ny), NZ)
-        y2 = lax.rem(y + lax.rem(r, ny), ny)
-        remote(
-            lrsend.at[place(x2, y2, z2)], lrbuf.at[own], asem.at[0], asem.at[1],
-            device(x2, y2, z2, c),
-        ).start()
-        return carry
-
-    lax.fori_loop(1, peers, send_channel, 0)
+    turns = sorted(range(nx), key=lambda k: -min(k, nx - k))
+
+    def send_channel(turn):
+        x2 = lax.rem(x + turn, nx)
+
+        def send(k, carry):
+            z2 = lax.rem(z + away(lax.div(k, ny), NZ), NZ)
+            y2 = lax.rem(y + away(lax.rem(k, ny), ny), ny)
+            remote(
+                lrsend.at[place(x2, y2, z2)], lrbuf.at[own], asem.at[0, turn], asem.at[1, turn],
+                device(x2, y2, z2, c),
+            ).start()
+            return carry
+
+        lax.fori_loop(0, ny * NZ - (turn == 0), send, 0)
+
+    for turn in turns:
+        send_channel(turn)
     lrbuf[own] = lrsend[own]
 
     for g in range(nx):
@@ -247,6 +255,82 @@
             remote(
                 usend.at[g], ubuf.at[y], usend_sem.at[g], urecv_sem.at[y], device(g, x, z, c)
             ).start()
+
+    group = lax.broadcasted_iota(jnp.int32, (zh * NC * ROWS, width), 1) // thirds
+    swaps = []
+    for turn in turns:
+        base = lax.rem(x + nx - turn, nx) * ny * NZ
+        arrived(lrbuf.at[pl.ds(0, ny * NZ - (turn == 0))], asem.at[1, turn])
+        part = pl.ds(base, ny * NZ)
+        swap = remote(
+            lrbuf.at[part], lrsib.at[part], ssem.at[0, turn], ssem.at[1, turn], sibling
+        )
+        swap.start()
+        swap.wait_recv()
+        swaps.append(swap)
+        for s in range(ny):
+            mine = lrbuf[pl.ds(base + s * NZ, NZ)].astype(F32)
+            other = lrsib[pl.ds(base + s * NZ, NZ)].astype(F32)
+            m0, m1 = jnp.where(first, mine, other), jnp.where(first, other, mine)
+            span = slice(s * width, (s + 1) * width)
+            rows = []
+            for z2 in range(NZ):
+                at = z2 % 2 * zh + z2 // 2
+                rows += [m0[at, ROWS:], m1[at, ROWS:]]
+            right = jnp.concatenate(rows, axis=0)
+            for m in range(nx):
+                rolled = pltpu.roll(right, m * thirds, 1) if m else right
+                rwide[m * width : (m + 1) * width, span] = rolled.astype(BF16)
+            rows = []
+            for m in (m0, m1):
+                rows.append(jnp.where(first, m[:zh, :ROWS], m[zh:, :ROWS]))
+            left = jnp.concatenate(rows, axis=1).reshape(zh * NC * ROWS, width)
+            for g in range(nx):
+                lwide[g * zh * NC * ROWS : (g + 1) * zh * NC * ROWS, span] = jnp.where(
+                    group == g, left, 0.0
+                ).astype(BF16)
+        if turn == turns[0]:
+            mixed[...] = nt(lwide[...], rwide[...])
+        else:
+            mixed[...] += nt(lwide[...], rwide[...])
+    for g in range(nx):
+        for m in range(nx):
+            g2 = (g - m) % nx
+            part = mixed[g * zh * NC * ROWS : (g + 1) * zh * NC * ROWS, m * width : (m + 1) * width]
+            msend[(g2 * nx + g) * zh : (g2 * nx + g + 1) * zh] = part.reshape(
+                zh, NC * ROWS, width
+            ).astype(BF16)
+
+    side = lax.rem(z, 2)
+    home = (x * ny + y) * zh + lax.div(z, 2)
+    stays = side == c
+
+    def send_back(turn, k):
+        x2 = lax.rem(x + turn, nx)
+        zh2 = lax.rem(lax.div(z, 2) + away(lax.div(k, ny), zh), zh)
+        y2 = lax.rem(y + away(lax.rem(k, ny), ny), ny)
+        remote(
+            msend.at[(y2 * nx + x2) * zh + zh2], mbuf.at[side, home],
+            msem.at[0, turn], msem.at[1, turn], device(x2, y2, 2 * zh2 + c, side),
+        ).start()
+
+    def send_group(turn, count):
+        def send(k, carry):
+            send_back(turn, k)
+            return carry
+
+        lax.fori_loop(0, count, send, 0)
+
+    for turn in turns:
+        send_group(turn, ny * zh - (turn == 0))
+
+    @pl.when(stays)
+    def _():
+        mbuf[side, home] = msend[(y * nx + x) * zh + lax.div(z, 2)]
+
+    @pl.when(jnp.logical_not(stays))
+    def _():
+        send_back(0, ny * zh - 1)
 
     for s in range(ny):
 
@@ -265,74 +349,27 @@
         norm = zscore(u, 1).astype(BF16)
         gates[i] = jax.nn.sigmoid(jnp.dot(norm, fg_v[...], preferred_element_type=F32))
 
-    arrived(lrbuf.at[pl.ds(0, peers - 1)], asem.at[1])
-    swaps = []
-    for s in range(ny):
-        part = pl.ds(s * nx * NZ, nx * NZ)
-        swaps.append(remote(lrbuf.at[part], lrsib.at[part], ssem.at[0, s], ssem.at[1, s], sibling))
-        swaps[-1].start()
-    group = lax.broadcasted_iota(jnp.int32, (zh * NC * ROWS, width), 1) // thirds
-    for s in range(nyx):
-        if s % nx == 0:
-            swaps[s // nx].wait_recv()
-        mine = lrbuf[s * NZ : (s + 1) * NZ].astype(F32)
-        other = lrsib[s * NZ : (s + 1) * NZ].astype(F32)
-        m0, m1 = jnp.where(first, mine, other), jnp.where(first, other, mine)
-        span = slice(s * width, (s + 1) * width)
-        rows = []
-        for z2 in range(NZ):
-            at = z2 % 2 * zh + z2 // 2
-            rows += [m0[at, ROWS:], m1[at, ROWS:]]
-        right = jnp.concatenate(rows, axis=0)
-        for m in range(nx):
-            rolled = pltpu.roll(right, m * thirds, 1) if m else right
-            rwide[m * width : (m + 1) * width, span] = rolled.astype(BF16)
-        rows = []
-        for m in (m0, m1):
-            rows.append(jnp.where(first, m[:zh, :ROWS], m[zh:, :ROWS]))
-        left = jnp.concatenate(rows, axis=1).reshape(zh * NC * ROWS, width)
-        for g in range(nx):
-            lwide[g * zh * NC * ROWS : (g + 1) * zh * NC * ROWS, span] = jnp.where(
-                group == g, left, 0.0
-            ).astype(BF16)
-    mixed = nt(lwide[...], rwide[...])
-    for g in range(nx):
-        for m in range(nx):
-            g2 = (g - m) % nx
-            part = mixed[g * zh * NC * ROWS : (g + 1) * zh * NC * ROWS, m * width : (m + 1) * width]
-            msend[(g2 * nx + g) * zh : (g2 * nx + g + 1) * zh] = part.reshape(
-                zh, NC * ROWS, width
-            ).astype(BF16)
-
-    side = lax.rem(z, 2)
-    home = (y * nx + x) * zh + lax.div(z, 2)
-
-    def send_back(k, carry):
-        x2 = lax.rem(x + lax.div(k, ny * zh), nx)
-        y2 = lax.rem(y + lax.rem(lax.div(k, zh), ny), ny)
-        zh2 = lax.rem(lax.div(z, 2) + lax.rem(k, zh), zh)
-        remote(
-            msend.at[(y2 * nx + x2) * zh + zh2], mbuf.at[side, home], msem.at[0], msem.at[1],
-            device(x2, y2, 2 * zh2 + c, side),
-        ).start()
-        return carry
-
-    stays = side == c
-    lax.fori_loop(1, nyx * zh, send_back, 0)
-
-    @pl.when(stays)
-    def _():
-        mbuf[side, home] = msend[home]
-        arrived(mbuf.at[c, pl.ds(0, nyx * zh - 1)], msem.at[1])
-
-    @pl.when(jnp.logical_not(stays))
-    def _():
-        send_back(0, 0)
-        arrived(mbuf.at[c], msem.at[1])
-
-    final = remote(mbuf.at[c], mbuf.at[c], fsem.at[0], fsem.at[1], sibling)
-    final.start()
-    final.wait_recv()
+    finals = []
+    for turn in turns:
+        base = lax.rem(x + nx - turn, nx) * ny * zh
+        if turn:
+            arrived(mbuf.at[c, pl.ds(0, ny * zh)], msem.at[1, turn])
+        else:
+
+            @pl.when(stays)
+            def _():
+                arrived(mbuf.at[c, pl.ds(0, ny * zh - 1)], msem.at[1, 0])
+
+            @pl.when(jnp.logical_not(stays))
+            def _():
+                arrived(mbuf.at[c, pl.ds(0, ny * zh)], msem.at[1, 0])
+
+        part = mbuf.at[c, pl.ds(base, ny * zh)]
+        final = remote(part, part, fsem.at[0, turn], fsem.at[1, turn], sibling)
+        final.start()
+        finals.append(final)
+    for final in finals:
+        final.wait_recv()
 
     full = mbuf[...].astype(F32)
     full = jnp.where(first, full[:, :, :ROWS], full[:, :, ROWS:])
@@ -360,19 +397,21 @@
         def _():
             arrived(usend.at[g], usend_sem.at[g])
 
-    arrived(lrbuf.at[pl.ds(0, peers - 1)], asem.at[0])
-    for swap in swaps:
-        swap.wait_send()
+    for turn in turns:
+        arrived(lrbuf.at[pl.ds(0, ny * NZ - (turn == 0))], asem.at[0, turn])
+        if turn:
+            arrived(msend.at[pl.ds(0, ny * zh)], msem.at[0, turn])
 
     @pl.when(stays)
     def _():
-        arrived(msend.at[pl.ds(0, nyx * zh - 1)], msem.at[0])
+        arrived(msend.at[pl.ds(0, ny * zh - 1)], msem.at[0, 0])
 
     @pl.when(jnp.logical_not(stays))
     def _():
-        arrived(msend, msem.at[0])
-
-    final.wait_send()
+        arrived(msend.at[pl.ds(0, ny * zh)], msem.at[0, 0])
+
+    for copy in swaps + finals:
+        copy.wait_send()
 
 
 def shards(msa, pair, wl, wr, wo, *weights):
@@ -410,8 +449,9 @@
         vmem((cz, 2 * ROWS, width), BF16),
         vmem((peers, 2 * ROWS, width), BF16),
         vmem((peers, 2 * ROWS, width), BF16),
-        vmem((nx * NZ * ROWS, ny * nx * width), BF16),
-        vmem((nx * width, ny * nx * width), BF16),
+        vmem((nx * NZ * ROWS, ny * width), BF16),
+        vmem((nx * width, ny * width), BF16),
+        vmem((nx * NZ * ROWS, nx * width), F32),
         vmem((peers // 2, 2 * ROWS, width), BF16),
         vmem((2, peers // 2, 2 * ROWS, width), BF16),
         vmem((cz * ROWS, width), F32),
@@ -429,10 +469,10 @@
         dma((2,)),
         dma((nx,)),
         dma((ny,)),
-        dma((2,)),
-        dma((2, ny)),
-        dma((2,)),
-        dma((2,)),
+        dma((2, nx)),
+        dma((2, nx)),
+        dma((2, nx)),
+        dma((2, nx)),
     ]
     return pl.pallas_call(
         functools.partial(kernel, nx, ny, ny * sd),

time: 66.3 us -> 63.6 us (0.959)
  Pallas kernels: 64.5 us -> 61.8 us
    pallas_call x1, Pallas kernels: 64.5 us -> 61.8 us  [shards(): pl.pallas_call(functools.partial(kernel, nx, ny, ny * sd), out_shape=jax....]
where the time goes in v4:
time: 63.6 us; the launch traced here: 63.5 us
  Pallas kernels  61.8 us (97%)
  local copies, waits for them, and re-layouts  1.67 us (3%)
    pallas_call x1, Pallas kernels, shards(): pl.pallas_call(functools.partial(kernel, nx, ny, ny * sd), out_shape=jax....  61.8 us
    unnamed x1, local copies, waits for them, and re-layouts  1.67 us

profile of v4, /device:TPU:1, one launch (start us, length us, event | category | flops | bytes accessed | tf_op | source)
XLA Modules:
  0.0 63.5 jit_solution(9753518717147028157)
XLA Ops:
  0.0 61.8 %shard_map.109 = bf16[8,128,128]{2,1,0:T(8,128)(2,1)} custom-call(bf16[1024,256]{1,0:T(8,128)(2,1)} %bitcast.3, bf16[8,512,128]{2,1,0:T(8,128)(2,1)} %pair_ref.1, bf16[32,256]{1,0:T(8,128)(2,1)} %bitcast.4, bf16[32,256]{1,0:T(8,128)(2,1)} %bitcast.5, bf16[1024,128]{1,0:T(8,128)(2,1)} %wo_ref.1, bf16[128,128]{1,0:T(8,128)(2,1)} %ag_ref.1, ...), custom_call_target="tpu_custom_call" | custom-call | tf_op jit(solution)/shard_map/pallas_call | solution.py:477
  61.8 1.7 %copy.13 = bf16[8,128,128]{2,1,0:T(8,128)(2,1)} copy(bf16[8,128,128]{2,1,0:T(8,128)(2,1)} %shard_map.109) | data formatting | bytes 524288

commit v5 on v4

--- a/solution.py
+++ b/solution.py
@@ -59,6 +59,18 @@
     def place(x1, y1, z1):
         return (x1 * ny + y1) * NZ + lax.rem(z1, 2) * zh + lax.div(z1, 2)
 
+    xs = [lax.rem(x + k, nx) for k in range(nx)]
+    ys = [lax.rem(y + k, ny) for k in range(ny)]
+    zs = [lax.rem(z + k, NZ) for k in range(NZ)]
+    xat = [v * (NZ * NC) + c for v in xs]
+    zat = [v * NC for v in zs]
+    xpart = [v * (ny * NZ) for v in xs]
+    ypart = [v * NZ for v in ys]
+    zpart = [place(0, 0, v) for v in zs]
+
+    def outward(n):
+        return sorted(range(n), key=lambda k: -min(k, n - k))
+
     def remote(source, target, send, recv, to):
         return pltpu.make_async_remote_copy(
             source, target, send, recv, device_id=to, device_id_type=MESH
@@ -75,14 +87,13 @@
     def greet(x2, y2, z2, c2):
         pl.semaphore_signal(barrier, inc=1, device_id=device(x2, y2, z2, c2), device_id_type=MESH)
 
-    def greet_yz(k, carry):
-        greet(x, lax.rem(y + lax.rem(k, ny), ny), lax.rem(z + lax.div(k, ny), NZ), c)
-        return carry
-
     greet(x, y, z, 1 - c)
     for k in range(1, nx):
         greet(lax.rem(x + k, nx), y, z, c)
-    lax.fori_loop(1, ny * NZ, greet_yz, 0)
+    for kz in (0, 1, 2, NZ - 2, NZ - 1):
+        for ky in range(ny):
+            if kz or ky:
+                greet(x, ys[ky], zs[kz], c)
 
     sources = (msa_ref, wl_ref, wr_ref, wo_ref, ag_ref, ap_ref, bg_ref, bp_ref, fg_ref, fp_ref)
     loads = [
@@ -110,9 +121,9 @@
         lscr[pl.ds(i, ch, stride=ROWS), :] = proj[:ch]
         rsend[i // jr, (i % jr) * ch : (i % jr + 1) * ch, :] = proj[ch:].astype(BF16)
     lbuf[y, x] = lscr[...].astype(BF16)
-    rbuf[c, y * NZ + z] = rsend[y]
-
-    pl.semaphore_wait(barrier, ny * NZ + nx - 1)
+    rbuf[c, y, z] = rsend[y]
+
+    pl.semaphore_wait(barrier, ny * 5 + nx - 1)
 
     half = ch * ROWS // 2
     low, high = pl.ds(0, half), pl.ds(half, half)
@@ -123,15 +134,13 @@
     for k in range(1, ny):
         remote(yfirst, yfirst, lsem.at[2], lsem.at[3], device(x, lax.rem(y + k, ny), z, c)).start()
 
-    def send_right(k, carry):
-        z2 = lax.rem(z + lax.div(k, ny), NZ)
-        y2 = lax.rem(y + lax.rem(k, ny), ny)
-        remote(
-            rsend.at[y2], rbuf.at[c, y * NZ + z], rsem.at[0], rsem.at[1], device(x, y2, z2, c)
-        ).start()
-        return carry
-
-    lax.fori_loop(1, ny * NZ, send_right, 0)
+    for kz, at in ((2, 0), (NZ - 2, 0), (1, 2), (NZ - 1, 2), (0, 6)):
+        for ky in range(ny):
+            if kz or ky:
+                remote(
+                    rsend.at[ys[ky]], rbuf.at[c, y, z], rsem.at[at], rsem.at[at + 1],
+                    (xat[0] + zat[kz], ys[ky]),
+                ).start()
 
     arrived(lbuf.at[0, pl.ds(0, nx - 1), low], lsem.at[1])
     ythen = lbuf.at[y, :, low]
@@ -141,6 +150,16 @@
     xthen = lbuf.at[:, x, high]
     for k in range(1, nx):
         remote(xthen, xthen, lsem.at[6], lsem.at[7], device(lax.rem(x + k, nx), y, z, c)).start()
+
+    arrived(rbuf.at[0, :, pl.ds(0, 2)], rsem.at[1])
+    early, late = pl.ds(0, ny // 2), pl.ds(ny // 2, ny // 2)
+    for part, kz in (
+        (rbuf.at[c, early, zs[NZ - 2]], 2),
+        (rbuf.at[c, late, zs[2]], NZ - 2),
+        (rbuf.at[c, :, zs[NZ - 2]], 1),
+        (rbuf.at[c, :, zs[2]], NZ - 1),
+    ):
+        remote(part, part, rsem.at[4], rsem.at[5], (xat[0] + zat[kz], y)).start()
 
     pair_copy.wait()
     columns = pairv.shape[1]
@@ -168,7 +187,9 @@
     for t, ref in enumerate((ag_v, ap_v, bg_v, bp_v)):
         wt4[t * cz : (t + 1) * cz, :] = ref[...].astype(F32).T.astype(BF16)
 
-    arrived(rbuf.at[0, pl.ds(0, ny * NZ - 1)], rsem.at[1])
+    arrived(rbuf.at[0, :, pl.ds(0, 2)], rsem.at[3])
+    arrived(rbuf.at[0, pl.ds(0, ny - 1), 0], rsem.at[7])
+    arrived(rbuf.at[0, :, pl.ds(0, NZ - 5)], rsem.at[5])
     cross = remote(rbuf.at[c], rbuf.at[c], csem.at[0], csem.at[1], sibling)
     cross.start()
     arrived(lbuf.at[pl.ds(0, ny - 1), :, low], lsem.at[5])
@@ -177,7 +198,7 @@
     def outer(side):
         right = rbuf[side]
         right = jnp.concatenate(
-            [right[s * NZ : (s + 1) * NZ].reshape(NZ * jr * ch, sd) for s in range(ny)], axis=1
+            [right[s].reshape(NZ * jr * ch, sd) for s in range(ny)], axis=1
         )
 
         def one(g, carry):
@@ -223,24 +244,15 @@
 
     own = place(x, y, z)
 
-    turns = sorted(range(nx), key=lambda k: -min(k, nx - k))
-
-    def send_channel(turn):
-        x2 = lax.rem(x + turn, nx)
-
-        def send(k, carry):
-            z2 = lax.rem(z + away(lax.div(k, ny), NZ), NZ)
-            y2 = lax.rem(y + away(lax.rem(k, ny), ny), ny)
-            remote(
-                lrsend.at[place(x2, y2, z2)], lrbuf.at[own], asem.at[0, turn], asem.at[1, turn],
-                device(x2, y2, z2, c),
-            ).start()
-            return carry
-
-        lax.fori_loop(0, ny * NZ - (turn == 0), send, 0)
-
+    turns = outward(nx)
     for turn in turns:
-        send_channel(turn)
+        for kz in outward(NZ):
+            for ky in outward(ny):
+                if turn or kz or ky:
+                    remote(
+                        lrsend.at[xpart[turn] + ypart[ky] + zpart[kz]], lrbuf.at[own],
+                        asem.at[0, turn], asem.at[1, turn], (xat[turn] + zat[kz], ys[ky]),
+                    ).start()
     lrbuf[own] = lrsend[own]
 
     for g in range(nx):
@@ -305,24 +317,23 @@
     home = (x * ny + y) * zh + lax.div(z, 2)
     stays = side == c
 
-    def send_back(turn, k):
-        x2 = lax.rem(x + turn, nx)
-        zh2 = lax.rem(lax.div(z, 2) + away(lax.div(k, ny), zh), zh)
-        y2 = lax.rem(y + away(lax.rem(k, ny), ny), ny)
+    zhs = [lax.rem(lax.div(z, 2) + k, zh) for k in range(zh)]
+    xback = [v * (NZ * NC) + side for v in xs]
+    zback = [v * (2 * NC) + c * NC for v in zhs]
+    ypart = [v * (nx * zh) for v in ys]
+    xpart = [v * zh for v in xs]
+
+    def send_back(turn, kz, ky):
         remote(
-            msend.at[(y2 * nx + x2) * zh + zh2], mbuf.at[side, home],
-            msem.at[0, turn], msem.at[1, turn], device(x2, y2, 2 * zh2 + c, side),
+            msend.at[ypart[ky] + xpart[turn] + zhs[kz]], mbuf.at[side, home],
+            msem.at[0, turn], msem.at[1, turn], (xback[turn] + zback[kz], ys[ky]),
         ).start()
 
-    def send_group(turn, count):
-        def send(k, carry):
-            send_back(turn, k)
-            return carry
-
-        lax.fori_loop(0, count, send, 0)
-
     for turn in turns:
-        send_group(turn, ny * zh - (turn == 0))
+        for kz in outward(zh):
+            for ky in outward(ny):
+                if turn or kz or ky:
+                    send_back(turn, kz, ky)
 
     @pl.when(stays)
     def _():
@@ -330,7 +341,7 @@
 
     @pl.when(jnp.logical_not(stays))
     def _():
-        send_back(0, ny * zh - 1)
+        send_back(0, 0, 0)
 
     for s in range(ny):
 
@@ -388,7 +399,10 @@
     arrived(lbuf.at[pl.ds(0, ny - 1), 0, high], lsem.at[2])
     arrived(lbuf.at[pl.ds(0, ny - 1), :, low], lsem.at[4])
     arrived(lbuf.at[:, pl.ds(0, nx - 1), high], lsem.at[6])
-    arrived(rbuf.at[0, pl.ds(0, ny * NZ - 1)], rsem.at[0])
+    arrived(rbuf.at[0, :, pl.ds(0, 2)], rsem.at[0])
+    arrived(rbuf.at[0, :, pl.ds(0, 2)], rsem.at[2])
+    arrived(rbuf.at[0, pl.ds(0, ny - 1), 0], rsem.at[6])
+    arrived(rbuf.at[0, :, pl.ds(0, NZ - 5)], rsem.at[4])
     arrived(psend.at[pl.ds(0, nx - 1)], psem.at[0])
     cross.wait_send()
     for g in range(nx):
@@ -432,7 +446,7 @@
         vmem((ch * ROWS, sd), F32),
         vmem((ny, nx, ch * ROWS, sd), BF16),
         vmem((ny, jr * ch, sd), BF16),
-        vmem((NC, ny * NZ, jr * ch, sd), BF16),
+        vmem((NC, ny, NZ, jr * ch, sd), BF16),
         vmem((NC * nx, step, 4 * ch * ch), BF16),
         vmem((4 * ch * ch, 4 * cz), BF16),
         vmem((ROWS, columns, cz), BF16),
@@ -463,8 +477,8 @@
     ] + [vmem((cz, cz), BF16)] * 6 + [
         dma((10,)),
         dma,
+        dma((10,)),
         dma((8,)),
-        dma((2,)),
         dma((2,)),
         dma((2,)),
         dma((nx,)),

time: 63.6 us -> 59.7 us (0.939)
  Pallas kernels: 61.8 us -> 57.9 us
    pallas_call x1, Pallas kernels: 61.8 us -> 57.9 us  [shards(): pl.pallas_call(functools.partial(kernel, nx, ny, ny * sd), out_shape=jax....]
where the time goes in v5:
time: 59.7 us; the launch traced here: 59.6 us
  Pallas kernels  57.9 us (97%)
  local copies, waits for them, and re-layouts  1.67 us (3%)
    pallas_call x1, Pallas kernels, shards(): pl.pallas_call(functools.partial(kernel, nx, ny, ny * sd), out_shape=jax....  57.9 us
    unnamed x1, local copies, waits for them, and re-layouts  1.67 us

profile of v5, /device:TPU:1, one launch (start us, length us, event | category | flops | bytes accessed | tf_op | source)
XLA Modules:
  0.0 59.6 jit_solution(6342376921878872171)
XLA Ops:
  0.0 57.9 %shard_map.109 = bf16[8,128,128]{2,1,0:T(8,128)(2,1)} custom-call(bf16[1024,256]{1,0:T(8,128)(2,1)} %bitcast.3, bf16[8,512,128]{2,1,0:T(8,128)(2,1)} %pair_ref.1, bf16[32,256]{1,0:T(8,128)(2,1)} %bitcast.4, bf16[32,256]{1,0:T(8,128)(2,1)} %bitcast.5, bf16[1024,128]{1,0:T(8,128)(2,1)} %wo_ref.1, bf16[128,128]{1,0:T(8,128)(2,1)} %ag_ref.1, ...), custom_call_target="tpu_custom_call" | custom-call | tf_op jit(solution)/shard_map/pallas_call | solution.py:491
  57.9 1.7 %copy.13 = bf16[8,128,128]{2,1,0:T(8,128)(2,1)} copy(bf16[8,128,128]{2,1,0:T(8,128)(2,1)} %shard_map.109) | data formatting | bytes 524288

commit v6 on v5

--- a/solution.py
+++ b/solution.py
@@ -35,7 +35,7 @@
     msa_ref, pair_ref, wl_ref, wr_ref, wo_ref, ag_ref, ap_ref, bg_ref, bp_ref, fg_ref, fp_ref,
     out_ref,
     xf, lscr, lbuf, rsend, rbuf, abuf, bd, pairv, pairf, pstage, psend, pbuf, usend, ubuf, vbuf, upd,
-    wt4, lrscr, lrsend, lrbuf, lrsib, lwide, rwide, mixed, msend, mbuf, nscr, gates,
+    wt4, norm, lrscr, lrsend, lrbuf, lrsib, lwide, rwide, mixed, msend, mbuf, nscr, gates,
     msa_v, wl_v, wr_v, wo_v, ag_v, ap_v, bg_v, bp_v, fg_v, fp_v,
     load_sem, pair_sem, lsem, rsem, csem, psem, usend_sem, urecv_sem, asem, ssem, msem, fsem,
 ):
@@ -234,18 +234,24 @@
         vbuf[g * thirds * ROWS : (g + 1) * thirds * ROWS] = u.astype(F32)
 
     for i in range(ROWS):
-        norm = zscore(vbuf[pl.ds(i, width, stride=ROWS), :], 1).astype(BF16)
-        four = nt(wt4[...], norm)
-        lrscr[pl.ds(i, cz, stride=2 * ROWS), :] = jax.nn.sigmoid(four[:cz]) * four[cz : 2 * cz]
-        lrscr[pl.ds(ROWS + i, cz, stride=2 * ROWS), :] = (
-            jax.nn.sigmoid(four[2 * cz : 3 * cz]) * four[3 * cz :]
+        norm[i * width : (i + 1) * width] = zscore(
+            vbuf[pl.ds(i, width, stride=ROWS), :], 1
+        ).astype(BF16)
+    own = place(x, y, z)
+    turns = outward(nx)
+    some = ny * NZ
+    for turn in turns:
+        weights = jnp.concatenate(
+            [wt4[pl.ds(pl.multiple_of(t * cz + xpart[turn], some), some)] for t in range(4)], axis=0
         )
-    lrsend[...] = lrscr[...].reshape(cz, 2 * ROWS, width).astype(BF16)
-
-    own = place(x, y, z)
-
-    turns = outward(nx)
-    for turn in turns:
+        four = nt(weights, norm[...])
+        lhs = jax.nn.sigmoid(four[:some]) * four[some : 2 * some]
+        rhs = jax.nn.sigmoid(four[2 * some : 3 * some]) * four[3 * some :]
+        for i in range(ROWS):
+            span = slice(i * width, (i + 1) * width)
+            lrscr[pl.ds(i, some, stride=2 * ROWS), :] = lhs[:, span]
+            lrscr[pl.ds(ROWS + i, some, stride=2 * ROWS), :] = rhs[:, span]
+        lrsend[pl.ds(xpart[turn], some)] = lrscr[...].reshape(some, 2 * ROWS, width).astype(BF16)
         for kz in outward(NZ):
             for ky in outward(ny):
                 if turn or kz or ky:
@@ -357,8 +363,8 @@
     for i in range(ROWS):
         u = vbuf[pl.ds(i, width, stride=ROWS), :]
         upd[i] = u
-        norm = zscore(u, 1).astype(BF16)
-        gates[i] = jax.nn.sigmoid(jnp.dot(norm, fg_v[...], preferred_element_type=F32))
+        unit = zscore(u, 1).astype(BF16)
+        gates[i] = jax.nn.sigmoid(jnp.dot(unit, fg_v[...], preferred_element_type=F32))
 
     finals = []
     for turn in turns:
@@ -384,15 +390,15 @@
 
     full = mbuf[...].astype(F32)
     full = jnp.where(first, full[:, :, :ROWS], full[:, :, ROWS:])
-    norm = zscore(full.reshape(cz, ROWS, width), 0)
+    unit = zscore(full.reshape(cz, ROWS, width), 0)
     for p in range(2):
         for s in range(nyx):
             start = s * NZ + p * zh
-            part = norm[(p * nyx + s) * zh : (p * nyx + s + 1) * zh]
+            part = unit[(p * nyx + s) * zh : (p * nyx + s + 1) * zh]
             nscr[start * ROWS : (start + zh) * ROWS] = part.reshape(zh * ROWS, width)
     for i in range(ROWS):
-        norm = nscr[pl.ds(i, cz, stride=ROWS), :].T.astype(BF16)
-        proj = jnp.dot(norm, fp_v[...], preferred_element_type=F32)
+        unit = nscr[pl.ds(i, cz, stride=ROWS), :].T.astype(BF16)
+        proj = jnp.dot(unit, fp_v[...], preferred_element_type=F32)
         out_ref[i] = (upd[i] + gates[i] * proj).astype(BF16)
 
     arrived(lbuf.at[0, pl.ds(0, nx - 1), low], lsem.at[0])
@@ -459,7 +465,8 @@
         vmem((width * ROWS, cz), F32),
         vmem((ROWS, width, cz), F32),
         vmem((4 * cz, cz), BF16),
-        vmem((cz * 2 * ROWS, width), F32),
+        vmem((ROWS * width, cz), BF16),
+        vmem((ny * NZ * 2 * ROWS, width), F32),
         vmem((cz, 2 * ROWS, width), BF16),
         vmem((peers, 2 * ROWS, width), BF16),
         vmem((peers, 2 * ROWS, width), BF16),

time: 59.7 us -> 59 us (0.988)
  Pallas kernels: 57.9 us -> 57.2 us
    pallas_call x1, Pallas kernels: 57.9 us -> 57.2 us  [shards(): pl.pallas_call(functools.partial(kernel, nx, ny, ny * sd), out_shape=jax....]
where the time goes in v6:
time: 59 us; the launch traced here: 58.9 us
  Pallas kernels  57.2 us (97%)
  local copies, waits for them, and re-layouts  1.67 us (3%)
    pallas_call x1, Pallas kernels, shards(): pl.pallas_call(functools.partial(kernel, nx, ny, ny * sd), out_shape=jax....  57.2 us
    unnamed x1, local copies, waits for them, and re-layouts  1.67 us

profile of v6, /device:TPU:1, one launch (start us, length us, event | category | flops | bytes accessed | tf_op | source)
XLA Modules:
  0.0 58.9 jit_solution(4735665212755048555)
XLA Ops:
  0.0 57.2 %shard_map.109 = bf16[8,128,128]{2,1,0:T(8,128)(2,1)} custom-call(bf16[1024,256]{1,0:T(8,128)(2,1)} %bitcast.3, bf16[8,512,128]{2,1,0:T(8,128)(2,1)} %pair_ref.1, bf16[32,256]{1,0:T(8,128)(2,1)} %bitcast.4, bf16[32,256]{1,0:T(8,128)(2,1)} %bitcast.5, bf16[1024,128]{1,0:T(8,128)(2,1)} %wo_ref.1, bf16[128,128]{1,0:T(8,128)(2,1)} %ag_ref.1, ...), custom_call_target="tpu_custom_call" | custom-call | tf_op jit(solution)/shard_map/pallas_call | solution.py:498
  57.2 1.7 %copy.13 = bf16[8,128,128]{2,1,0:T(8,128)(2,1)} copy(bf16[8,128,128]{2,1,0:T(8,128)(2,1)} %shard_map.109) | data formatting | bytes 524288

commit v7 on v6

--- a/solution.py
+++ b/solution.py
@@ -366,6 +366,27 @@
         unit = zscore(u, 1).astype(BF16)
         gates[i] = jax.nn.sigmoid(jnp.dot(unit, fg_v[...], preferred_element_type=F32))
 
+    arrived(lbuf.at[0, pl.ds(0, nx - 1), low], lsem.at[0])
+    arrived(lbuf.at[pl.ds(0, ny - 1), 0, high], lsem.at[2])
+    arrived(lbuf.at[pl.ds(0, ny - 1), :, low], lsem.at[4])
+    arrived(lbuf.at[:, pl.ds(0, nx - 1), high], lsem.at[6])
+    arrived(rbuf.at[0, :, pl.ds(0, 2)], rsem.at[0])
+    arrived(rbuf.at[0, :, pl.ds(0, 2)], rsem.at[2])
+    arrived(rbuf.at[0, pl.ds(0, ny - 1), 0], rsem.at[6])
+    arrived(rbuf.at[0, :, pl.ds(0, NZ - 5)], rsem.at[4])
+    arrived(psend.at[pl.ds(0, nx - 1)], psem.at[0])
+    cross.wait_send()
+    for g in range(nx):
+
+        @pl.when(jnp.logical_not(jnp.logical_and(x == g, y == x)))
+        def _():
+            arrived(usend.at[g], usend_sem.at[g])
+
+    for turn in turns:
+        arrived(lrbuf.at[pl.ds(0, ny * NZ - (turn == 0))], asem.at[0, turn])
+    for copy in swaps:
+        copy.wait_send()
+
     finals = []
     for turn in turns:
         base = lax.rem(x + nx - turn, nx) * ny * zh
@@ -401,24 +422,7 @@
         proj = jnp.dot(unit, fp_v[...], preferred_element_type=F32)
         out_ref[i] = (upd[i] + gates[i] * proj).astype(BF16)
 
-    arrived(lbuf.at[0, pl.ds(0, nx - 1), low], lsem.at[0])
-    arrived(lbuf.at[pl.ds(0, ny - 1), 0, high], lsem.at[2])
-    arrived(lbuf.at[pl.ds(0, ny - 1), :, low], lsem.at[4])
-    arrived(lbuf.at[:, pl.ds(0, nx - 1), high], lsem.at[6])
-    arrived(rbuf.at[0, :, pl.ds(0, 2)], rsem.at[0])
-    arrived(rbuf.at[0, :, pl.ds(0, 2)], rsem.at[2])
-    arrived(rbuf.at[0, pl.ds(0, ny - 1), 0], rsem.at[6])
-    arrived(rbuf.at[0, :, pl.ds(0, NZ - 5)], rsem.at[4])
-    arrived(psend.at[pl.ds(0, nx - 1)], psem.at[0])
-    cross.wait_send()
-    for g in range(nx):
-
-        @pl.when(jnp.logical_not(jnp.logical_and(x == g, y == x)))
-        def _():
-            arrived(usend.at[g], usend_sem.at[g])
-
     for turn in turns:
-        arrived(lrbuf.at[pl.ds(0, ny * NZ - (turn == 0))], asem.at[0, turn])
         if turn:
             arrived(msend.at[pl.ds(0, ny * zh)], msem.at[0, turn])
 
@@ -430,7 +434,7 @@
     def _():
         arrived(msend.at[pl.ds(0, ny * zh)], msem.at[0, 0])
 
-    for copy in swaps + finals:
+    for copy in finals:
         copy.wait_send()
 
 
@@ -497,14 +501,14 @@
     ]
     return pl.pallas_call(
         functools.partial(kernel, nx, ny, ny * sd),
-        out_shape=jax.ShapeDtypeStruct((ROWS, width, cz), BF16),
+        out_shape=pltpu.VMEM((ROWS, width, cz), BF16),
         in_specs=[pl.BlockSpec(memory_space=pltpu.HBM)] * 11,
         out_specs=pl.BlockSpec(memory_space=pltpu.VMEM),
         scratch_shapes=scratch,
         compiler_params=pltpu.CompilerParams(
-            collective_id=0, has_side_effects=True, vmem_limit_bytes=60 * 2**20
+            collective_id=0, has_side_effects=True, vmem_limit_bytes=48 * 2**20
         ),
-    )(msa.reshape(sd * ROWS, cm), pair, wl.T, wr.T, wo, *weights)
+    )(*[pltpu.with_memory_space_constraint(v, pltpu.HBM) for v in (msa.reshape(sd * ROWS, cm), pair, wl.T, wr.T, wo, *weights)])
 
 
 def solution(mesh):

time: 59 us -> 57.3 us (0.971)
  local copies, waits for them, and re-layouts: 1.67 us -> 0.71 us
  Pallas kernels: 57.2 us -> 56.5 us
    unnamed x1, local copies, waits for them, and re-layouts: 1.67 us -> 0.71 us
    pallas_call x1, Pallas kernels: 57.2 us -> 56.5 us  [shards(): pl.pallas_call(functools.partial(kernel, nx, ny, ny * sd), out_shape=pltp...]
where the time goes in v7:
time: 57.3 us; the launch traced here: 57.2 us
  Pallas kernels  56.5 us (99%)
  local copies, waits for them, and re-layouts  0.71 us (1%)
    pallas_call x1, Pallas kernels, shards(): pl.pallas_call(functools.partial(kernel, nx, ny, ny * sd), out_shape=pltp...  56.5 us

profile of v7, /device:TPU:1, one launch (start us, length us, event | category | flops | bytes accessed | tf_op | source)
XLA Modules:
  0.0 57.2 jit_solution(10939356925117077999)
XLA Ops:
  0.0 56.5 %shard_map.109 = bf16[8,128,128]{2,1,0:T(8,128)(2,1)S(1)} custom-call(bf16[1024,256]{1,0:T(8,128)(2,1)} %bitcast.3, bf16[8,512,128]{2,1,0:T(8,128)(2,1)} %pair_ref.1, bf16[32,256]{1,0:T(8,128)(2,1)} %bitcast.4, bf16[32,256]{1,0:T(8,128)(2,1)} %bitcast.5, bf16[1024,128]{1,0:T(8,128)(2,1)} %wo_ref.1, bf16[128,128]{1,0:T(8,128)(2,1)} %ag_ref.1, ...), custom_call_target="tpu_custom_call" | custom-call | tf_op jit(solution)/shard_map/pallas_call | solution.py:502
  56.5 0.7 %copy.13 = bf16[8,128,128]{2,1,0:T(8,128)(2,1)} copy(bf16[8,128,128]{2,1,0:T(8,128)(2,1)S(1)} %shard_map.109) | data formatting | bytes 524288

commit v8 on v7

--- a/solution.py
+++ b/solution.py
@@ -120,7 +120,7 @@
         proj = nt(wlr, v)
         lscr[pl.ds(i, ch, stride=ROWS), :] = proj[:ch]
         rsend[i // jr, (i % jr) * ch : (i % jr + 1) * ch, :] = proj[ch:].astype(BF16)
-    lbuf[y, x] = lscr[...].astype(BF16)
+    lbuf[y, x] = lscr[: ch * ROWS].astype(BF16)
     rbuf[c, y, z] = rsend[y]
 
     pl.semaphore_wait(barrier, ny * 5 + nx - 1)
@@ -163,7 +163,7 @@
 
     pair_copy.wait()
     columns = pairv.shape[1]
-    pairf[...] = pairv[...].astype(F32).reshape(ROWS * columns, cz)
+    pairf[: ROWS * columns] = pairv[...].astype(F32).reshape(ROWS * columns, cz)
     for i in range(ROWS):
         for h in range(NC):
             for r in range(jr):
@@ -171,7 +171,8 @@
                 for g in range(nx):
                     start = (g * thirds + h * NZ * jr + r) * ROWS + i
                     pstage[pl.ds(start, NZ, stride=jr * ROWS), :] = v[g * NZ : (g + 1) * NZ]
-    psend[...] = pstage[...].astype(BF16).reshape(nx, thirds * ROWS, cz)
+    staged = pstage[: nx * thirds * ROWS].astype(BF16)
+    psend[...] = staged.reshape(nx, thirds * ROWS, cz)
     pbuf[x] = psend[x]
     for k in range(1, nx):
         x2 = lax.rem(x + k, nx)
@@ -251,7 +252,8 @@
             span = slice(i * width, (i + 1) * width)
             lrscr[pl.ds(i, some, stride=2 * ROWS), :] = lhs[:, span]
             lrscr[pl.ds(ROWS + i, some, stride=2 * ROWS), :] = rhs[:, span]
-        lrsend[pl.ds(xpart[turn], some)] = lrscr[...].reshape(some, 2 * ROWS, width).astype(BF16)
+        tiles = lrscr[: some * 2 * ROWS].reshape(some, 2 * ROWS, width)
+        lrsend[pl.ds(xpart[turn], some)] = tiles.astype(BF16)
         for kz in outward(NZ):
             for ky in outward(ny):
                 if turn or kz or ky:
@@ -452,25 +454,25 @@
     vmem = pltpu.VMEM
     dma = pltpu.SemaphoreType.DMA
     scratch = [
-        vmem((cm // 128 * sd * ROWS, 128), F32),
-        vmem((ch * ROWS, sd), F32),
+        vmem((cm // 128 * sd * ROWS + ROWS, 128), F32),
+        vmem((ch * ROWS + ROWS, sd), F32),
         vmem((ny, nx, ch * ROWS, sd), BF16),
         vmem((ny, jr * ch, sd), BF16),
         vmem((NC, ny, NZ, jr * ch, sd), BF16),
         vmem((NC * nx, step, 4 * ch * ch), BF16),
         vmem((4 * ch * ch, 4 * cz), BF16),
         vmem((ROWS, columns, cz), BF16),
-        vmem((ROWS * columns, cz), F32),
-        vmem((nx * thirds * ROWS, cz), F32),
+        vmem((ROWS * columns + 2 * ROWS, cz), F32),
+        vmem((nx * thirds * ROWS + 2 * ROWS, cz), F32),
         vmem((nx, thirds * ROWS, cz), BF16),
         vmem((nx, thirds * ROWS, cz), BF16),
         vmem((nx, thirds * ROWS, cz), BF16),
         vmem((ny, thirds * ROWS, cz), BF16),
-        vmem((width * ROWS, cz), F32),
+        vmem((width * ROWS + ROWS, cz), F32),
         vmem((ROWS, width, cz), F32),
         vmem((4 * cz, cz), BF16),
         vmem((ROWS * width, cz), BF16),
-        vmem((ny * NZ * 2 * ROWS, width), F32),
+        vmem((ny * NZ * 2 * ROWS + 2 * ROWS, width), F32),
         vmem((cz, 2 * ROWS, width), BF16),
         vmem((peers, 2 * ROWS, width), BF16),
         vmem((peers, 2 * ROWS, width), BF16),
@@ -479,7 +481,7 @@
         vmem((nx * NZ * ROWS, nx * width), F32),
         vmem((peers // 2, 2 * ROWS, width), BF16),
         vmem((2, peers // 2, 2 * ROWS, width), BF16),
-        vmem((cz * ROWS, width), F32),
+        vmem((cz * ROWS + ROWS, width), F32),
         vmem((ROWS, width, cz), F32),
         vmem((sd * ROWS, cm), BF16),
         vmem((ch, cm), BF16),

time: 57.3 us -> 57.4 us (level)
  no operation moved by 1% of the time
where the time goes in v8:
time: 57.4 us; the launch traced here: 57.3 us
  Pallas kernels  56.6 us (99%)
  local copies, waits for them, and re-layouts  0.71 us (1%)
    pallas_call x1, Pallas kernels, shards(): pl.pallas_call(functools.partial(kernel, nx, ny, ny * sd), out_shape=pltp...  56.6 us

profile of v8, /device:TPU:1, one launch (start us, length us, event | category | flops | bytes accessed | tf_op | source)
XLA Modules:
  0.0 57.3 jit_solution(1916373203582570933)
XLA Ops:
  0.0 56.6 %shard_map.109 = bf16[8,128,128]{2,1,0:T(8,128)(2,1)S(1)} custom-call(bf16[1024,256]{1,0:T(8,128)(2,1)} %bitcast.3, bf16[8,512,128]{2,1,0:T(8,128)(2,1)} %pair_ref.1, bf16[32,256]{1,0:T(8,128)(2,1)} %bitcast.4, bf16[32,256]{1,0:T(8,128)(2,1)} %bitcast.5, bf16[1024,128]{1,0:T(8,128)(2,1)} %wo_ref.1, bf16[128,128]{1,0:T(8,128)(2,1)} %ag_ref.1, ...), custom_call_target="tpu_custom_call" | custom-call | tf_op jit(solution)/shard_map/pallas_call | solution.py:504
  56.6 0.7 %copy.13 = bf16[8,128,128]{2,1,0:T(8,128)(2,1)} copy(bf16[8,128,128]{2,1,0:T(8,128)(2,1)S(1)} %shard_map.109) | data formatting | bytes 524288

commit v9 on v8

--- a/solution.py
+++ b/solution.py
@@ -142,25 +142,6 @@
                     (xat[0] + zat[kz], ys[ky]),
                 ).start()
 
-    arrived(lbuf.at[0, pl.ds(0, nx - 1), low], lsem.at[1])
-    ythen = lbuf.at[y, :, low]
-    for k in range(1, ny):
-        remote(ythen, ythen, lsem.at[4], lsem.at[5], device(x, lax.rem(y + k, ny), z, c)).start()
-    arrived(lbuf.at[pl.ds(0, ny - 1), 0, high], lsem.at[3])
-    xthen = lbuf.at[:, x, high]
-    for k in range(1, nx):
-        remote(xthen, xthen, lsem.at[6], lsem.at[7], device(lax.rem(x + k, nx), y, z, c)).start()
-
-    arrived(rbuf.at[0, :, pl.ds(0, 2)], rsem.at[1])
-    early, late = pl.ds(0, ny // 2), pl.ds(ny // 2, ny // 2)
-    for part, kz in (
-        (rbuf.at[c, early, zs[NZ - 2]], 2),
-        (rbuf.at[c, late, zs[2]], NZ - 2),
-        (rbuf.at[c, :, zs[NZ - 2]], 1),
-        (rbuf.at[c, :, zs[2]], NZ - 1),
-    ):
-        remote(part, part, rsem.at[4], rsem.at[5], (xat[0] + zat[kz], y)).start()
-
     pair_copy.wait()
     columns = pairv.shape[1]
     pairf[: ROWS * columns] = pairv[...].astype(F32).reshape(ROWS * columns, cz)
@@ -177,6 +158,25 @@
     for k in range(1, nx):
         x2 = lax.rem(x + k, nx)
         remote(psend.at[x2], pbuf.at[x], psem.at[0], psem.at[1], device(x2, y, z, c)).start()
+
+    arrived(lbuf.at[0, pl.ds(0, nx - 1), low], lsem.at[1])
+    ythen = lbuf.at[y, :, low]
+    for k in range(1, ny):
+        remote(ythen, ythen, lsem.at[4], lsem.at[5], device(x, lax.rem(y + k, ny), z, c)).start()
+    arrived(lbuf.at[pl.ds(0, ny - 1), 0, high], lsem.at[3])
+    xthen = lbuf.at[:, x, high]
+    for k in range(1, nx):
+        remote(xthen, xthen, lsem.at[6], lsem.at[7], device(lax.rem(x + k, nx), y, z, c)).start()
+
+    arrived(rbuf.at[0, :, pl.ds(0, 2)], rsem.at[1])
+    early, late = pl.ds(0, ny // 2), pl.ds(ny // 2, ny // 2)
+    for part, kz in (
+        (rbuf.at[c, early, zs[NZ - 2]], 2),
+        (rbuf.at[c, late, zs[2]], NZ - 2),
+        (rbuf.at[c, :, zs[NZ - 2]], 1),
+        (rbuf.at[c, :, zs[2]], NZ - 1),
+    ):
+        remote(part, part, rsem.at[4], rsem.at[5], (xat[0] + zat[kz], y)).start()
 
     for load in loads[3:]:
         load.wait()

time: 57.4 us -> 57.2 us (level)
  no operation moved by 1% of the time
where the time goes in v9:
time: 57.2 us; the launch traced here: 57.1 us
  Pallas kernels  56.4 us (99%)
  local copies, waits for them, and re-layouts  0.71 us (1%)
    pallas_call x1, Pallas kernels, shards(): pl.pallas_call(functools.partial(kernel, nx, ny, ny * sd), out_shape=pltp...  56.4 us

profile of v9, /device:TPU:1, one launch (start us, length us, event | category | flops | bytes accessed | tf_op | source)
XLA Modules:
  0.0 57.1 jit_solution(14913742537300035257)
XLA Ops:
  0.0 56.4 %shard_map.109 = bf16[8,128,128]{2,1,0:T(8,128)(2,1)S(1)} custom-call(bf16[1024,256]{1,0:T(8,128)(2,1)} %bitcast.3, bf16[8,512,128]{2,1,0:T(8,128)(2,1)} %pair_ref.1, bf16[32,256]{1,0:T(8,128)(2,1)} %bitcast.4, bf16[32,256]{1,0:T(8,128)(2,1)} %bitcast.5, bf16[1024,128]{1,0:T(8,128)(2,1)} %wo_ref.1, bf16[128,128]{1,0:T(8,128)(2,1)} %ag_ref.1, ...), custom_call_target="tpu_custom_call" | custom-call | tf_op jit(solution)/shard_map/pallas_call | solution.py:504
  56.4 0.7 %copy.13 = bf16[8,128,128]{2,1,0:T(8,128)(2,1)} copy(bf16[8,128,128]{2,1,0:T(8,128)(2,1)S(1)} %shard_map.109) | data formatting | bytes 524288

commit v10 on v9

--- a/solution.py
+++ b/solution.py
@@ -254,8 +254,8 @@
             lrscr[pl.ds(ROWS + i, some, stride=2 * ROWS), :] = rhs[:, span]
         tiles = lrscr[: some * 2 * ROWS].reshape(some, 2 * ROWS, width)
         lrsend[pl.ds(xpart[turn], some)] = tiles.astype(BF16)
-        for kz in outward(NZ):
-            for ky in outward(ny):
+        for ky in outward(ny):
+            for kz in outward(NZ):
                 if turn or kz or ky:
                     remote(
                         lrsend.at[xpart[turn] + ypart[ky] + zpart[kz]], lrbuf.at[own],

time: 57.2 us -> 57.4 us (level)
  no operation moved by 1% of the time
where the time goes in v10:
time: 57.4 us; the launch traced here: 57.3 us
  Pallas kernels  56.6 us (99%)
  local copies, waits for them, and re-layouts  0.71 us (1%)
    pallas_call x1, Pallas kernels, shards(): pl.pallas_call(functools.partial(kernel, nx, ny, ny * sd), out_shape=pltp...  56.6 us

profile of v10, /device:TPU:1, one launch (start us, length us, event | category | flops | bytes accessed | tf_op | source)
XLA Modules:
  0.0 57.3 jit_solution(4197099850896513295)
XLA Ops:
  0.0 56.6 %shard_map.109 = bf16[8,128,128]{2,1,0:T(8,128)(2,1)S(1)} custom-call(bf16[1024,256]{1,0:T(8,128)(2,1)} %bitcast.3, bf16[8,512,128]{2,1,0:T(8,128)(2,1)} %pair_ref.1, bf16[32,256]{1,0:T(8,128)(2,1)} %bitcast.4, bf16[32,256]{1,0:T(8,128)(2,1)} %bitcast.5, bf16[1024,128]{1,0:T(8,128)(2,1)} %wo_ref.1, bf16[128,128]{1,0:T(8,128)(2,1)} %ag_ref.1, ...), custom_call_target="tpu_custom_call" | custom-call | tf_op jit(solution)/shard_map/pallas_call | solution.py:504
  56.6 0.7 %copy.13 = bf16[8,128,128]{2,1,0:T(8,128)(2,1)} copy(bf16[8,128,128]{2,1,0:T(8,128)(2,1)S(1)} %shard_map.109) | data formatting | bytes 524288
